TPU v7x, 32 devices: a whole 2x2x4 slice. The times are simulated.
32 devices in a mesh: context: 4 (over y, core), experts: 8 (over z, x).
Axes of the slice: x: 2, y: 2, z: 4, core: 2. Of those that a mesh axis runs over, the one named last changes fastest.
Arguments:
- tokens: bfloat16 [4096, 2048], P(('context', 'experts')), may hold values from -6 to 6
- attn_gain: bfloat16 [2048], P(('context', 'experts')), may hold values from 0.5 to 1.5
- query_key_value_weight: bfloat16 [2048, 3072], P(('context', 'experts')), may hold values from -0.125 to 0.125
- out_weight: bfloat16 [2048, 2048], P(('context', 'experts')), may hold values from -3 to 3
- ffn_gain: bfloat16 [2048], P(('context', 'experts')), may hold values from 0.5 to 1.5
- router_weight: bfloat16 [2048, 16], P(('context', 'experts')), may hold values from -0.0625 to 0.0625
- shared_gate: bfloat16 [2048, 2816], P(('context', 'experts')), may hold values from -0.125 to 0.125
- shared_up: bfloat16 [2048, 2816], P(('context', 'experts')), may hold values from -0.125 to 0.125
- shared_down: bfloat16 [2816, 2048], P(('context', 'experts')), may hold values from -0.109375 to 0.109375
- routed_gate_weight: bfloat16 [16, 2048, 1408], P('experts'), may hold values from -0.125 to 0.125
- routed_up_weight: bfloat16 [16, 2048, 1408], P('experts'), may hold values from -0.125 to 0.125
- routed_down_weight: bfloat16 [16, 1408, 2048], P('experts'), may hold values from -0.875 to 0.875
- routes: int32 [4096, 6], P(('context', 'experts')), may hold values from 0 to 15, all different within a row; in each aligned block of 128 rows (0 to 127, 128 to 255, ...) at most 64 rows name the same one
- cotangent: bfloat16 [4096, 2048], P(('context', 'experts')), may hold values from -6 to 6
Outputs:
- layer_out: bfloat16 [4096, 2048], P(('context', 'experts'))
- tokens_grad: float32 [4096, 2048], P(('context', 'experts'))
- attn_gain_grad: float32 [2048], P(('context', 'experts'))
- qkv_weight_grad: float32 [2048, 3072], P(('context', 'experts'))
- out_weight_grad: float32 [2048, 2048], P(('context', 'experts'))
- ffn_gain_grad: float32 [2048], P(('context', 'experts'))
- router_weight_grad: float32 [2048, 16], P(('context', 'experts'))
- shared_gate_grad: float32 [2048, 2816], P(('context', 'experts'))
- shared_up_grad: float32 [2048, 2816], P(('context', 'experts'))
- shared_down_grad: float32 [2816, 2048], P(('context', 'experts'))
- expert_gate_grad: float32 [16, 2048, 1408], P('experts', 'context')
- expert_up_grad: float32 [16, 2048, 1408], P('experts', 'context')
- expert_down_grad: float32 [16, 1408, 2048], P('experts', None, 'context')
Inputs may be any that keep to these rules, and one draw needn't show every extreme that they name: `routes`: each token names 6 different experts. In the 128 rows of one device no expert is named by more than 64 rows, a bound that some block reaches.
All inputs are finite; a program needn't handle non-finite values.
Results may differ from a plain program's by a relative error of at most 0.025.
Values may be sent and summed in bfloat16 or wider, within the bound.
No kernel may reach another device: no remote copies, remote signals or barrier semaphores. Data moves between devices by JAX's collectives and lax.ppermute only.
A program may use at most 512 MiB of HBM per device.

v0:
```python
import math

import jax
import jax.numpy as jnp
from jax import lax
from jax.sharding import PartitionSpec as P

QUERY_HEADS = 16
KEY_VALUE_HEADS = 4
HEAD_DIM = 128
TOP = 6


EPSILON = 1e-06
THETA = 10000.0
NEG_LARGE = -1e30


def rms_scale(values):
    return lax.rsqrt(jnp.mean(values * values, axis=-1, keepdims=True) + EPSILON)


def rotate_halves(values, token_position, direction):
    half_width = values.shape[-1] // 2
    frequency = THETA ** (-jnp.arange(half_width, dtype=jnp.float32) * 2.0 / values.shape[-1])
    angles = token_position[:, None] * frequency[None, :]
    cosine = jnp.cos(angles)[:, None, :]
    sine_part = direction * jnp.sin(angles)[:, None, :]
    first = values[..., :half_width]
    second = values[..., half_width:]
    return jnp.concatenate(
        [first * cosine - second * sine_part, second * cosine + first * sine_part], axis=-1
    )


def norm_back(values, row_scale, gain_values, grad_out):
    weighted = grad_out * gain_values
    gain_grad = jnp.sum(grad_out * values * row_scale, axis=0)
    inner_mean = jnp.mean(weighted * values, axis=-1, keepdims=True)
    return (
        row_scale * weighted - values * row_scale * row_scale * row_scale * inner_mean,
        gain_grad,
    )


def inner_rows(left, right):
    return lax.dot_general(
        left, right, (((0,), (0,)), ((), ())), preferred_element_type=jnp.float32
    )


def dot_last(left, right):
    return lax.dot_general(
        left, right, (((1,), (1,)), ((), ())), preferred_element_type=jnp.float32
    )


def gather_dense(shards):
    return (
        lax.all_gather(shards[0], ("context", "experts"), axis=0, tiled=True),
        lax.all_gather(shards[1], ("context", "experts"), axis=0, tiled=True),
        lax.all_gather(shards[2], ("context", "experts"), axis=0, tiled=True),
        lax.all_gather(shards[3], ("context", "experts"), axis=0, tiled=True),
        lax.all_gather(shards[4], ("context", "experts"), axis=0, tiled=True),
        lax.all_gather(shards[5], ("context", "experts"), axis=0, tiled=True),
        lax.all_gather(shards[6], ("context", "experts"), axis=0, tiled=True),
        lax.all_gather(shards[7], ("context", "experts"), axis=0, tiled=True),
    )


def attention_forward(query_rows, key_block, value_block, my_start):
    row_count = query_rows.shape[0]
    head_count = query_rows.shape[1]
    score_scale = query_rows.shape[2] ** (-0.5)
    query_pos = my_start + jnp.arange(row_count, dtype=jnp.int32)
    my_last = my_start + row_count - 1

    def fold_keys(state_in, shard_pair, first_row):
        key_piece, value_piece = shard_pair
        length = key_piece.shape[0]
        tile_width = math.gcd(length, 512)

        def tile_step(tile_index, state):
            offset = tile_index * tile_width

            def tile_work(running):
                run_max, run_sum, weighted_sum = running
                key_tile = lax.dynamic_slice_in_dim(key_piece, offset, tile_width, 0)
                value_tile = lax.dynamic_slice_in_dim(value_piece, offset, tile_width, 0)
                scores = (
                    jnp.einsum(
                        "iqh,jh->iqj", query_rows, key_tile, preferred_element_type=jnp.float32
                    )
                    * score_scale
                )
                key_pos = offset + jnp.arange(tile_width, dtype=jnp.int32)
                visible = (query_pos[:, None] >= key_pos[None, :])[:, None, :]
                scores = jnp.where(visible, scores, NEG_LARGE)
                new_max = jnp.maximum(run_max, jnp.max(scores, axis=-1))
                weights = jnp.where(visible, jnp.exp(scores - new_max[:, :, None]), 0.0)
                rescale = jnp.exp(run_max - new_max)
                run_sum = run_sum * rescale + jnp.sum(weights, axis=-1)
                weighted_sum = weighted_sum * rescale[:, :, None] + jnp.einsum(
                    "iqj,jh->iqh",
                    weights.astype(jnp.bfloat16),
                    value_tile,
                    preferred_element_type=jnp.float32,
                )
                return (new_max, run_sum, weighted_sum)

            return lax.cond(offset <= my_last, tile_work, lambda running: running, state)

        return lax.fori_loop(0, length // tile_width, tile_step, state_in)

    initial = (
        jnp.full((row_count, head_count), NEG_LARGE, jnp.float32),
        jnp.zeros((row_count, head_count), jnp.float32),
        jnp.zeros(query_rows.shape, jnp.float32),
    )
    run_max, run_sum, weighted_sum = fold_keys(
        initial,
        (
            lax.all_gather(key_block, "context", axis=0, tiled=True),
            lax.all_gather(value_block, "context", axis=0, tiled=True),
        ),
        jnp.int32(0),
    )
    return (weighted_sum / run_sum[:, :, None], run_max + jnp.log(run_sum))


def attention_backward(
    query_rows, key_block, value_block, grad_heads, log_total, row_delta, my_start
):
    row_count = query_rows.shape[0]
    score_scale = query_rows.shape[2] ** (-0.5)
    query_pos = my_start + jnp.arange(row_count, dtype=jnp.int32)
    my_last = my_start + row_count - 1
    total_keys = lax.axis_size("context") * row_count

    def fold_keys(state_in, shard_pair, first_row):
        key_piece, value_piece = shard_pair
        length = key_piece.shape[0]
        tile_width = math.gcd(length, 512)

        def tile_step(tile_index, state):
            offset = tile_index * tile_width

            def tile_work(running):
                query_grad, key_grad, value_grad = running
                key_tile = lax.dynamic_slice_in_dim(key_piece, offset, tile_width, 0)
                value_tile = lax.dynamic_slice_in_dim(value_piece, offset, tile_width, 0)
                scores = (
                    jnp.einsum(
                        "iqh,jh->iqj", query_rows, key_tile, preferred_element_type=jnp.float32
                    )
                    * score_scale
                )
                key_pos = offset + jnp.arange(tile_width, dtype=jnp.int32)
                visible = (query_pos[:, None] >= key_pos[None, :])[:, None, :]
                scores = jnp.where(visible, scores, NEG_LARGE)
                weights = jnp.where(visible, jnp.exp(scores - log_total[:, :, None]), 0.0)
                value_part = jnp.einsum(
                    "iqj,iqh->jh",
                    weights.astype(jnp.bfloat16),
                    grad_heads,
                    preferred_element_type=jnp.float32,
                )
                weight_grad = jnp.einsum(
                    "iqh,jh->iqj", grad_heads, value_tile, preferred_element_type=jnp.float32
                )
                score_grad = (weights * (weight_grad - row_delta[:, :, None])).astype(jnp.bfloat16)
                query_grad = (
                    query_grad
                    + jnp.einsum(
                        "iqj,jh->iqh", score_grad, key_tile, preferred_element_type=jnp.float32
                    )
                    * score_scale
                )
                key_part = (
                    jnp.einsum(
                        "iqj,iqh->jh", score_grad, query_rows, preferred_element_type=jnp.float32
                    )
                    * score_scale
                )
                key_old = lax.dynamic_slice_in_dim(key_grad, offset, tile_width, 0)
                key_grad = lax.dynamic_update_slice_in_dim(key_grad, key_old + key_part, offset, 0)
                value_old = lax.dynamic_slice_in_dim(value_grad, offset, tile_width, 0)
                value_grad = lax.dynamic_update_slice_in_dim(
                    value_grad, value_old + value_part, offset, 0
                )
                return (query_grad, key_grad, value_grad)

            return lax.cond(offset <= my_last, tile_work, lambda running: running, state)

        return lax.fori_loop(0, length // tile_width, tile_step, state_in)

    head_width = query_rows.shape[2]
    initial = (
        jnp.zeros(query_rows.shape, jnp.float32),
        jnp.zeros((total_keys, head_width), jnp.float32),
        jnp.zeros((total_keys, head_width), jnp.float32),
    )
    query_grad, key_full, value_full = fold_keys(
        initial,
        (
            lax.all_gather(key_block, "context", axis=0, tiled=True),
            lax.all_gather(value_block, "context", axis=0, tiled=True),
        ),
        jnp.int32(0),
    )
    key_grad, value_grad = (
        lax.psum_scatter(
            key_full.astype(jnp.bfloat16), "context", scatter_dimension=0, tiled=True
        ).astype(jnp.float32),
        lax.psum_scatter(
            value_full.astype(jnp.bfloat16), "context", scatter_dimension=0, tiled=True
        ).astype(jnp.float32),
    )
    return (query_grad, key_grad, value_grad)


def body(
    tokens,
    attn_gain,
    query_key_value_weight,
    out_weight,
    ffn_gain,
    router_weight,
    shared_gate,
    shared_up,
    shared_down,
    routed_gate_weight,
    routed_up_weight,
    routed_down_weight,
    routes,
    cotangent,
):
    spread_rows = lax.axis_size("experts")
    token_count = tokens.shape[0]
    model_width = tokens.shape[1]
    local_experts = routed_gate_weight.shape[0]
    experts_all = local_experts * spread_rows
    query_width = QUERY_HEADS * HEAD_DIM
    key_width = KEY_VALUE_HEADS * HEAD_DIM
    repeat_times = spread_rows // KEY_VALUE_HEADS
    head_share = QUERY_HEADS // spread_rows
    dense_full = gather_dense(
        (
            attn_gain,
            query_key_value_weight,
            out_weight,
            ffn_gain,
            router_weight,
            shared_gate,
            shared_up,
            shared_down,
        )
    )
    gain_one, qkv_full, out_full, gain_two, router_full, gate_full, up_full, down_full = dense_full
    inputs = tokens.astype(jnp.float32)
    token_position = (
        lax.axis_index(("context", "experts")) * token_count
        + jnp.arange(token_count, dtype=jnp.int32)
    ).astype(jnp.float32)
    scale_one = rms_scale(inputs)
    normed_one = (inputs * scale_one * gain_one.astype(jnp.float32)).astype(jnp.bfloat16)
    projected_rows = jnp.dot(normed_one, qkv_full, preferred_element_type=jnp.float32)
    query_tok = rotate_halves(
        projected_rows[:, :query_width].reshape(token_count, QUERY_HEADS, HEAD_DIM),
        token_position,
        1.0,
    )
    key_tok = rotate_halves(
        projected_rows[:, query_width : query_width + key_width].reshape(
            token_count, KEY_VALUE_HEADS, HEAD_DIM
        ),
        token_position,
        1.0,
    )
    value_token = projected_rows[:, query_width + key_width :].reshape(
        token_count, KEY_VALUE_HEADS, HEAD_DIM
    )
    query_send = query_tok.reshape(token_count, spread_rows, head_share * HEAD_DIM).astype(
        jnp.bfloat16
    )
    key_send = jnp.repeat(key_tok, repeat_times, axis=1).astype(jnp.bfloat16)
    value_send = jnp.repeat(value_token, repeat_times, axis=1).astype(jnp.bfloat16)
    query_heads, key_heads, value_heads = (
        lax.all_to_all(query_send, "experts", split_axis=1, concat_axis=0, tiled=True),
        lax.all_to_all(key_send, "experts", split_axis=1, concat_axis=0, tiled=True),
        lax.all_to_all(value_send, "experts", split_axis=1, concat_axis=0, tiled=True),
    )
    row_count = token_count * spread_rows
    query_rows = query_heads.reshape(row_count, head_share, HEAD_DIM)
    key_block = key_heads.reshape(row_count, HEAD_DIM)
    value_block = value_heads.reshape(row_count, HEAD_DIM)
    my_start = lax.axis_index("context") * row_count
    attended, log_total = attention_forward(query_rows, key_block, value_block, my_start)
    attended_send = attended.reshape(row_count, 1, head_share * HEAD_DIM).astype(jnp.bfloat16)
    attended_tok = lax.all_to_all(
        attended_send, "experts", split_axis=0, concat_axis=1, tiled=True
    ).reshape(token_count, query_width)
    middle = inputs + jnp.dot(attended_tok, out_full, preferred_element_type=jnp.float32)
    scale_two = rms_scale(middle)
    normed_two = (middle * scale_two * gain_two.astype(jnp.float32)).astype(jnp.bfloat16)
    logits = jnp.dot(normed_two, router_full, preferred_element_type=jnp.float32)
    router_probs = jax.nn.softmax(logits, axis=-1)
    picked = (routes[:, :, None] == jnp.arange(experts_all, dtype=jnp.int32)[None, None, :]).astype(
        jnp.float32
    )
    gate_values = jnp.sum(picked * router_probs[:, None, :], axis=-1)
    shared_pre_gate = jnp.dot(normed_two, gate_full, preferred_element_type=jnp.float32)
    shared_pre_up = jnp.dot(normed_two, up_full, preferred_element_type=jnp.float32)
    shared_sigmoid = jax.nn.sigmoid(shared_pre_gate)
    shared_act = (shared_pre_gate * shared_sigmoid * shared_pre_up).astype(jnp.bfloat16)
    shared_out = jnp.dot(shared_act, down_full, preferred_element_type=jnp.float32)
    flat_ids = routes.reshape(-1)
    capacity = token_count * TOP * 4 // (3 * experts_all)
    onehot = (flat_ids[:, None] == jnp.arange(experts_all, dtype=jnp.int32)[None, :]).astype(
        jnp.int32
    )
    slot_index = jnp.sum((jnp.cumsum(onehot, axis=0) - onehot) * onehot, axis=1)
    target = flat_ids * capacity + slot_index

    def to_experts(row_values):
        buffer = (
            jnp.zeros((experts_all * capacity, model_width), row_values.dtype)
            .at[target]
            .set(row_values)
        )
        return buffer.reshape(spread_rows, local_experts, capacity, model_width)

    sent_rows = to_experts(jnp.repeat(normed_two, TOP, axis=0))
    received = lax.all_to_all(sent_rows, "experts", split_axis=0, concat_axis=2, tiled=True)
    expert_row_set = received.reshape(local_experts, spread_rows * capacity, model_width)
    pre_gate = jnp.einsum(
        "hbs,hst->hbt", expert_row_set, routed_gate_weight, preferred_element_type=jnp.float32
    )
    up_input = jnp.einsum(
        "hbs,hst->hbt", expert_row_set, routed_up_weight, preferred_element_type=jnp.float32
    )
    gate_sigmoid = jax.nn.sigmoid(pre_gate)
    activated_rows = (pre_gate * gate_sigmoid * up_input).astype(jnp.bfloat16)
    expert_result = jnp.einsum(
        "tqv,tvg->tqg", activated_rows, routed_down_weight, preferred_element_type=jnp.float32
    ).astype(jnp.bfloat16)
    returned = lax.all_to_all(
        expert_result.reshape(1, local_experts, spread_rows * capacity, model_width),
        "experts",
        split_axis=2,
        concat_axis=0,
        tiled=True,
    )
    picked_out = (
        returned.reshape(experts_all * capacity, model_width)[target]
        .reshape(token_count, TOP, model_width)
        .astype(jnp.float32)
    )
    block_out = middle + shared_out + jnp.sum(gate_values[:, :, None] * picked_out, axis=1)
    grad_final = cotangent.astype(jnp.float32)
    shared_dout = grad_final.astype(jnp.bfloat16)
    gate_grad = jnp.sum(picked_out * grad_final[:, None, :], axis=-1)
    routed_dy = (
        (gate_values[:, :, None] * grad_final[:, None, :])
        .astype(jnp.bfloat16)
        .reshape(token_count * TOP, model_width)
    )
    gradient_rows = lax.all_to_all(
        to_experts(routed_dy), "experts", split_axis=0, concat_axis=2, tiled=True
    ).reshape(local_experts, spread_rows * capacity, model_width)
    act_grad = jnp.einsum(
        "byi,bpi->byp", gradient_rows, routed_down_weight, preferred_element_type=jnp.float32
    )
    gate_input_gradient = (
        act_grad * up_input * gate_sigmoid * (1.0 + pre_gate * (1.0 - gate_sigmoid))
    ).astype(jnp.bfloat16)
    up_input_gradient = (act_grad * pre_gate * gate_sigmoid).astype(jnp.bfloat16)
    down_portion = jnp.einsum(
        "whn,wha->wna", activated_rows, gradient_rows, preferred_element_type=jnp.float32
    )
    gate_part = jnp.einsum(
        "vnm,vng->vmg", expert_row_set, gate_input_gradient, preferred_element_type=jnp.float32
    )
    up_part = jnp.einsum(
        "vnm,vng->vmg", expert_row_set, up_input_gradient, preferred_element_type=jnp.float32
    )
    row_grad = jnp.einsum(
        "jpz,jnz->jpn", gate_input_gradient, routed_gate_weight, preferred_element_type=jnp.float32
    ) + jnp.einsum(
        "jpz,jnz->jpn", up_input_gradient, routed_up_weight, preferred_element_type=jnp.float32
    )
    back_rows = lax.all_to_all(
        row_grad.reshape(1, local_experts, spread_rows * capacity, model_width).astype(
            jnp.bfloat16
        ),
        "experts",
        split_axis=2,
        concat_axis=0,
        tiled=True,
    ).astype(jnp.float32)
    routed_input_grad = jnp.sum(
        back_rows.reshape(experts_all * capacity, model_width)[target].reshape(
            token_count, TOP, model_width
        ),
        axis=1,
    )
    expert_gate_grad, expert_up_grad, expert_down_grad = (
        lax.psum_scatter(
            gate_part.astype(jnp.bfloat16), "context", scatter_dimension=1, tiled=True
        ).astype(jnp.float32),
        lax.psum_scatter(
            up_part.astype(jnp.bfloat16), "context", scatter_dimension=1, tiled=True
        ).astype(jnp.float32),
        lax.psum_scatter(
            down_portion.astype(jnp.bfloat16), "context", scatter_dimension=2, tiled=True
        ).astype(jnp.float32),
    )
    dense_back = gather_dense(
        (
            attn_gain,
            query_key_value_weight,
            out_weight,
            ffn_gain,
            router_weight,
            shared_gate,
            shared_up,
            shared_down,
        )
    )
    gain_one_back, qkv_back, out_back, gain_two_back, router_back, gate_back, up_back, down_back = (
        dense_back
    )
    shared_down_grad = inner_rows(shared_act, shared_dout)
    shared_act_grad = dot_last(shared_dout, down_back)
    shared_gate_pre_grad = (
        shared_act_grad
        * shared_pre_up
        * shared_sigmoid
        * (1.0 + shared_pre_gate * (1.0 - shared_sigmoid))
    ).astype(jnp.bfloat16)
    shared_up_pre_grad = (shared_act_grad * shared_pre_gate * shared_sigmoid).astype(jnp.bfloat16)
    shared_gate_grad = inner_rows(normed_two, shared_gate_pre_grad)
    shared_up_grad = inner_rows(normed_two, shared_up_pre_grad)
    prob_grad = jnp.sum(picked * gate_grad[:, :, None], axis=1)
    logit_grad = (
        router_probs * (prob_grad - jnp.sum(router_probs * prob_grad, axis=-1, keepdims=True))
    ).astype(jnp.bfloat16)
    router_weight_grad = inner_rows(normed_two, logit_grad)
    normed_grad = (
        routed_input_grad
        + dot_last(shared_gate_pre_grad, gate_back)
        + dot_last(shared_up_pre_grad, up_back)
        + dot_last(logit_grad, router_back)
    )
    middle_norm_grad, ffn_gain_grad = norm_back(
        middle, scale_two, gain_two_back.astype(jnp.float32), normed_grad
    )
    middle_grad = grad_final + middle_norm_grad
    branch_grad = middle_grad.astype(jnp.bfloat16)
    out_weight_grad = inner_rows(attended_tok, branch_grad)
    attended_grad = dot_last(branch_grad, out_back).astype(jnp.bfloat16)
    grad_heads = lax.all_to_all(
        attended_grad.reshape(token_count, spread_rows, head_share * HEAD_DIM),
        "experts",
        split_axis=1,
        concat_axis=0,
        tiled=True,
    ).reshape(row_count, head_share, HEAD_DIM)
    row_delta = jnp.sum(grad_heads.astype(jnp.float32) * attended, axis=-1)
    query_grad, key_grad, value_grad = attention_backward(
        query_rows, key_block, value_block, grad_heads, log_total, row_delta, my_start
    )
    query_back, key_backward, value_backward = (
        lax.all_to_all(
            query_grad.reshape(row_count, 1, head_share * HEAD_DIM).astype(jnp.bfloat16),
            "experts",
            split_axis=0,
            concat_axis=1,
            tiled=True,
        ).astype(jnp.float32),
        lax.all_to_all(
            key_grad.reshape(row_count, 1, HEAD_DIM).astype(jnp.bfloat16),
            "experts",
            split_axis=0,
            concat_axis=1,
            tiled=True,
        ).astype(jnp.float32),
        lax.all_to_all(
            value_grad.reshape(row_count, 1, HEAD_DIM).astype(jnp.bfloat16),
            "experts",
            split_axis=0,
            concat_axis=1,
            tiled=True,
        ).astype(jnp.float32),
    )
    query_pre = rotate_halves(
        query_back.reshape(token_count, QUERY_HEADS, HEAD_DIM), token_position, -1.0
    ).reshape(token_count, query_width)
    key_pre = rotate_halves(
        jnp.sum(key_backward.reshape(token_count, KEY_VALUE_HEADS, repeat_times, HEAD_DIM), axis=2),
        token_position,
        -1.0,
    ).reshape(token_count, key_width)
    value_before = jnp.sum(
        value_backward.reshape(token_count, KEY_VALUE_HEADS, repeat_times, HEAD_DIM), axis=2
    ).reshape(token_count, key_width)
    projected_grad = jnp.concatenate([query_pre, key_pre, value_before], axis=1).astype(
        jnp.bfloat16
    )
    qkv_weight_grad = inner_rows(normed_one, projected_grad)
    normed_one_grad = dot_last(projected_grad, qkv_back)
    input_norm_grad, attn_gain_grad = norm_back(
        inputs, scale_one, gain_one_back.astype(jnp.float32), normed_one_grad
    )
    tokens_grad = middle_grad + input_norm_grad
    summed = (
        lax.psum_scatter(attn_gain_grad, ("context", "experts"), scatter_dimension=0, tiled=True),
        lax.psum_scatter(qkv_weight_grad, ("context", "experts"), scatter_dimension=0, tiled=True),
        lax.psum_scatter(out_weight_grad, ("context", "experts"), scatter_dimension=0, tiled=True),
        lax.psum_scatter(ffn_gain_grad, ("context", "experts"), scatter_dimension=0, tiled=True),
        lax.psum_scatter(
            router_weight_grad, ("context", "experts"), scatter_dimension=0, tiled=True
        ),
        lax.psum_scatter(shared_gate_grad, ("context", "experts"), scatter_dimension=0, tiled=True),
        lax.psum_scatter(shared_up_grad, ("context", "experts"), scatter_dimension=0, tiled=True),
        lax.psum_scatter(shared_down_grad, ("context", "experts"), scatter_dimension=0, tiled=True),
    )
    return (
        block_out.astype(jnp.bfloat16),
        tokens_grad,
        summed[0],
        summed[1],
        summed[2],
        summed[3],
        summed[4],
        summed[5],
        summed[6],
        summed[7],
        expert_gate_grad,
        expert_up_grad,
        expert_down_grad,
    )


def solution(mesh):
    return jax.shard_map(
        body,
        mesh=mesh,
        in_specs=(
            P(("context", "experts"), None),
            P(("context", "experts")),
            P(("context", "experts"), None),
            P(("context", "experts"), None),
            P(("context", "experts")),
            P(("context", "experts"), None),
            P(("context", "experts"), None),
            P(("context", "experts"), None),
            P(("context", "experts"), None),
            P("experts", None, None),
            P("experts", None, None),
            P("experts", None, None),
            P(("context", "experts"), None),
            P(("context", "experts"), None),
        ),
        out_specs=(
            P(("context", "experts"), None),
            P(("context", "experts"), None),
            P(("context", "experts")),
            P(("context", "experts"), None),
            P(("context", "experts"), None),
            P(("context", "experts")),
            P(("context", "experts"), None),
            P(("context", "experts"), None),
            P(("context", "experts"), None),
            P(("context", "experts"), None),
            P("experts", "context", None),
            P("experts", "context", None),
            P("experts", None, "context"),
        ),
        check_vma=False,
    )
```

profile of v0, /device:TPU:10, one launch (start us, length us, event | category | flops | bytes accessed | tf_op | source)
XLA Modules:
  0.0 3632.1 jit_solution(13440088338940211093)
XLA Ops:
  9.7 42.1 %all-reduce.5 = (bf16[2048]{0:T(1024)(128)(2,1)S(1)}, bf16[2048]{0:T(1024)(128)(2,1)S(1)}) all-reduce(bf16[2048]{0:T(1024)(128)(2,1)S(1)} %dynamic-update-slice, bf16[2048]{0:T(1024)(128)(2,1)S(1)} %dynamic-update-slice.1), channel_id=1, replica_groups=mesh['context'=4,'experts'=8] {'context','experts'}, use_global_device_ids=true, to_apply=%add | all-reduce | flops 4096 | bytes 16384
  54.1 54.6 %all-gather.9.cloned.1.call-done = bf16[2048,3072]{1,0:T(8,128)(2,1)} async-done(((bf16[64,3072]{1,0:T(8,128)(2,1)}), bf16[2048,3072]{1,0:T(8,128)(2,1)}) %all-gather.9.cloned.1.call-update) | async-done | bytes 12582928 | tf_op jit(solution)/shard_map/all_gather | solution.py:61
  115.9 12.1 all_to_all.156
  128.2 12.4 all_to_all.157
  163.5 12.7 while.36
  197.1 49.6 %all-gather.15.cloned.1.call-done = bf16[2048,2048]{1,0:T(8,128)(2,1)} async-done(((bf16[64,2048]{1,0:T(8,128)(2,1)}), bf16[2048,2048]{1,0:T(8,128)(2,1)}) %all-gather.15.cloned.1.call-update) | async-done | bytes 8388624 | tf_op jit(solution)/shard_map/all_gather | solution.py:62
  289.9 178.3 %all-gather = bf16[32,64,16]{1,2,0:T(8,128)(2,1)S(1)} all-gather(bf16[1,64,16]{1,2,0:T(8,128)(2,1)S(1)} %bitcast.266), channel_id=1, replica_groups=mesh['context'=4,'experts'=8] {'context','experts'}, dimensions={0}, use_global_device_ids=true | all-gather | bytes 67584 | tf_op jit(solution)/shard_map/all_gather | solution.py:64
  469.5 15.6 scatter_custom_fusion.1
  500.6 116.3 %all-to-all-done.6 = bf16[8,2,64,2048]{3,2,1,0:T(8,128)(2,1)} async-done(((bf16[8,2,64,2048]{3,2,1,0:T(8,128)(2,1)}), bf16[8,2,64,2048]{3,2,1,0:T(8,128)(2,1)}, u32[]{:S(2)}, u32[]{:S(2)}) %all-to-all-start.6) | async-done | bytes 4194336 | tf_op jit(solution)/shard_map/all_to_all | solution.py:368
  621.9 12.8 fusion.99
  643.2 17.8 multiply_convert_fusion.1
  660.9 12.1 convert_bitcast_fusion
  688.5 12.5 fusion.101
  701.0 14.0 fusion.57
  723.6 54.9 %all-to-all-done.5 = bf16[1,2,512,2048]{3,1,0,2:T(2,128)(2,1)} async-done(((bf16[1,2,512,2048]{3,1,0,2:T(2,128)(2,1)}), bf16[1,2,512,2048]{3,1,0,2:T(2,128)(2,1)}, u32[]{:S(2)}, u32[]{:S(2)}) %all-to-all-start.5) | async-done | bytes 4194336 | tf_op jit(solution)/shard_map/all_to_all | solution.py:347
  834.1 41.6 %all-to-all-done.7 = bf16[1,2,512,2048]{3,1,0,2:T(2,128)(2,1)} async-done(((bf16[1,2,512,2048]{3,1,0,2:T(2,128)(2,1)}), bf16[1,2,512,2048]{3,1,0,2:T(2,128)(2,1)}, u32[]{:S(2)}, u32[]{:S(2)}) %all-to-all-start.7) | async-done | bytes 4194336 | tf_op jit(solution)/shard_map/all_to_all | solution.py:392
  967.5 24.5 while.37
  967.7 12.1 conditional.7
  979.8 12.0 conditional.7
  998.9 11.9 convolution_convert_fusion.2
  1010.9 12.1 convolution_convert_fusion.1
  1101.8 16.7 reduce-scatter.14.cloned.1.call-done
  1156.2 93.4 %reduce-scatter.34.cloned.1.call-done = f32[64,16]{1,0:T(8,128)} async-done(((f32[2048,16]{1,0:T(8,128)}), f32[64,16]{1,0:T(8,128)}) %reduce-scatter.34.cloned.1.call-update) | async-done | bytes 4112
  1260.1 47.7 %all-reduce.4 = (f32[2048]{0:T(1024)S(1)}, f32[2048]{0:T(1024)S(1)}) all-reduce(f32[2048]{0:T(1024)S(1)} %get-tuple-element.674, f32[2048]{0:T(1024)S(1)} %copy-done.39), channel_id=4, replica_groups=mesh['context'=4,'experts'=8] {'context','experts'}, use_global_device_ids=true, to_apply=%region_33.34.clone | all-reduce | flops 4096 | bytes 32768
  1310.3 38.6 %reduce-scatter.28.cloned.1.call-done = bf16[2,512,1408]{2,1,0:T(8,128)(2,1)} async-done(((bf16[2,2048,1408]{2,1,0:T(8,128)(2,1)}), bf16[2,512,1408]{2,1,0:T(8,128)(2,1)}) %reduce-scatter.28.cloned.1.call-update) | async-done | bytes 2883600 | tf_op jit(solution)/shard_map/reduce_scatter | solution.py:408
  1353.6 90.1 %reduce-scatter.30.cloned.1.call-done = bf16[2,512,1408]{2,1,0:T(8,128)(2,1)} async-done(((bf16[2,2048,1408]{2,1,0:T(8,128)(2,1)}), bf16[2,512,1408]{2,1,0:T(8,128)(2,1)}) %reduce-scatter.30.cloned.1.call-update) | async-done | bytes 2883600 | tf_op jit(solution)/shard_map/reduce_scatter | solution.py:411
  1448.4 90.2 %reduce-scatter.32.cloned.1.call-done = bf16[2,1408,512]{2,1,0:T(8,128)(2,1)} async-done(((bf16[2,1408,2048]{2,1,0:T(8,128)(2,1)}), bf16[2,1408,512]{2,1,0:T(8,128)(2,1)}) %reduce-scatter.32.cloned.1.call-update) | async-done | bytes 2883600 | tf_op jit(solution)/shard_map/reduce_scatter | solution.py:414
  1543.8 485.6 %reduce-scatter.22.cloned.1.call-done = f32[64,2816]{1,0:T(8,128)} async-done(((f32[2048,2816]{1,0:T(8,128)}), f32[64,2816]{1,0:T(8,128)}) %reduce-scatter.22.cloned.1.call-update) | async-done | bytes 720912 | tf_op jit(solution)/shard_map/reduce_scatter | solution.py:524
  2029.5 490.9 %reduce-scatter.24.cloned.1.call-done = f32[64,2816]{1,0:T(8,128)} async-done(((f32[2048,2816]{1,0:T(8,128)}), f32[64,2816]{1,0:T(8,128)}) %reduce-scatter.24.cloned.1.call-update) | async-done | bytes 720912 | tf_op jit(solution)/shard_map/reduce_scatter | solution.py:525
  2520.4 490.9 %reduce-scatter.26.cloned.1.call-done = f32[88,2048]{1,0:T(8,128)} async-done(((f32[2816,2048]{1,0:T(8,128)}), f32[88,2048]{1,0:T(8,128)}) %reduce-scatter.26.cloned.1.call-update) | async-done | bytes 720912 | tf_op jit(solution)/shard_map/reduce_scatter | solution.py:526
  3011.3 359.4 %reduce-scatter.20.cloned.1.call-done = f32[64,2048]{1,0:T(8,128)} async-done(((f32[2048,2048]{1,0:T(8,128)}), f32[64,2048]{1,0:T(8,128)}) %reduce-scatter.20.cloned.1.call-update) | async-done | bytes 524304 | tf_op jit(solution)/shard_map/reduce_scatter | solution.py:519
  3370.7 254.4 %reduce-scatter.18.cloned.1.call-done = f32[64,3072]{1,0:T(8,128)} async-done(((f32[2048,3072]{1,0:T(8,128)}), f32[64,3072]{1,0:T(8,128)}) %reduce-scatter.18.cloned.1.call-update) | async-done | bytes 786448 | tf_op jit(solution)/shard_map/reduce_scatter | solution.py:518
  (385 shorter events, 499.1 us)
Async XLA Ops:
  7.2 101.5 %all-gather.9.cloned.1.call-start = ((), (), s32[]{:S(2)}) async-start(), calls=%async_computation.23 | async-start | bytes 12976128 | tf_op jit(solution)/shard_map/all_gather | solution.py:61
  7.9 153.3 %all-gather.11.cloned.1.call-start = ((), (), s32[]{:S(2)}) async-start(), calls=%async_computation.24 | async-start | bytes 1310720 | tf_op jit(solution)/shard_map/all_gather | solution.py:123
  52.6 90.2 %copy-start.27 = (f32[128,64]{0,1:T(8,128)}, f32[128,64]{0,1:T(8,128)S(1)}, u32[]{:S(2)}) copy-start(f32[128,64]{0,1:T(8,128)S(1)} %get-tuple-element.744) | copy-start | bytes 98308
  128.1 35.4 all-gather.13.cloned.1.call-start
  140.6 106.1 %all-gather.15.cloned.1.call-start = ((), (), s32[]{:S(2)}) async-start(), calls=%async_computation.26 | async-start | bytes 8650752 | tf_op jit(solution)/shard_map/all_gather | solution.py:62
  141.2 645.5 %all-gather.17.cloned.1.call-start = ((), (), s32[]{:S(2)}) async-start(), calls=%async_computation.27 | async-start | bytes 11894784 | tf_op jit(solution)/shard_map/all_gather | solution.py:65
  141.8 652.0 %all-gather.19.cloned.1.call-start = ((), (), s32[]{:S(2)}) async-start(), calls=%async_computation.28 | async-start | bytes 11894784 | tf_op jit(solution)/shard_map/all_gather | solution.py:66
  143.8 16.6 all-to-all-start.1
  180.3 16.0 all-to-all-start.3
  272.1 213.0 %all-to-all-start.4 = ((bf16[8,2,64,2048]{3,2,1,0:T(8,128)(2,1)}), bf16[8,2,64,2048]{3,2,1,0:T(8,128)(2,1)}, u32[]{:S(2)}, u32[]{:S(2)}) async-start(bf16[8,2,64,2048]{3,2,1,0:T(8,128)(2,1)} %bitcast.232), calls=%async_computation.4 | async-start | bytes 8388608 | tf_op jit(solution)/shard_map/all_to_all | solution.py:334
  485.2 131.7 %all-to-all-start.6 = ((bf16[8,2,64,2048]{3,2,1,0:T(8,128)(2,1)}), bf16[8,2,64,2048]{3,2,1,0:T(8,128)(2,1)}, u32[]{:S(2)}, u32[]{:S(2)}) async-start(bf16[8,2,64,2048]{3,2,1,0:T(8,128)(2,1)} %bitcast.233), calls=%async_computation.6 | async-start | bytes 8388608 | tf_op jit(solution)/shard_map/all_to_all | solution.py:368
  495.0 305.8 %all-gather.21.cloned.1.call-start = ((), (), s32[]{:S(2)}) async-start(), calls=%async_computation.29 | async-start | bytes 11894784 | tf_op jit(solution)/shard_map/all_gather | solution.py:67
  681.5 96.9 %all-to-all-start.5 = ((bf16[1,2,512,2048]{3,1,0,2:T(2,128)(2,1)}), bf16[1,2,512,2048]{3,1,0,2:T(2,128)(2,1)}, u32[]{:S(2)}, u32[]{:S(2)}) async-start(bf16[1,2,512,2048]{3,1,0,2:T(2,128)(2,1)} %copy.290), calls=%async_computation.5 | async-start | bytes 8388608 | tf_op jit(solution)/shard_map/all_to_all | solution.py:347
  778.5 97.3 %all-to-all-start.7 = ((bf16[1,2,512,2048]{3,1,0,2:T(2,128)(2,1)}), bf16[1,2,512,2048]{3,1,0,2:T(2,128)(2,1)}, u32[]{:S(2)}, u32[]{:S(2)}) async-start(bf16[1,2,512,2048]{3,1,0,2:T(2,128)(2,1)} %copy.294), calls=%async_computation.7 | async-start | bytes 8388608 | tf_op jit(solution)/shard_map/all_to_all | solution.py:392
  810.9 106.8 %copy-start.15 = (bf16[128,2816]{1,0:T(8,128)(2,1)}, bf16[128,2816]{1,0:T(8,128)(2,1)S(1)}, u32[]{:S(2)}) copy-start(bf16[128,2816]{1,0:T(8,128)(2,1)S(1)} %get-tuple-element.730) | copy-start | bytes 2162692
  810.9 114.9 %copy-start.14 = (bf16[128,2816]{1,0:T(8,128)(2,1)}, bf16[128,2816]{1,0:T(8,128)(2,1)S(1)}, u32[]{:S(2)}) copy-start(bf16[128,2816]{1,0:T(8,128)(2,1)S(1)} %get-tuple-element.729) | copy-start | bytes 2162692
  939.6 18.4 all-to-all-start.8
  946.6 143.7 %reduce-scatter.16.cloned.1.call-start = ((), (), s32[]{:S(2)}) async-start(), calls=%async_computation.31 | async-start | bytes 1310720 | tf_op jit(solution)/shard_map/reduce_scatter | solution.py:215
  994.7 123.8 %reduce-scatter.14.cloned.1.call-start = ((), (), s32[]{:S(2)}) async-start(), calls=%async_computation.30 | async-start | bytes 1310720 | tf_op jit(solution)/shard_map/reduce_scatter | solution.py:212
  997.5 252.2 %reduce-scatter.34.cloned.1.call-start = ((), (), s32[]{:S(2)}) async-start(), calls=%async_computation.40 | async-start | bytes 1081344
  998.8 350.0 %reduce-scatter.28.cloned.1.call-start = ((), (), s32[]{:S(2)}) async-start(), calls=%async_computation.37 | async-start | bytes 14417920 | tf_op jit(solution)/shard_map/reduce_scatter | solution.py:408
  1010.9 432.8 %reduce-scatter.30.cloned.1.call-start = ((), (), s32[]{:S(2)}) async-start(), calls=%async_computation.38 | async-start | bytes 14417920 | tf_op jit(solution)/shard_map/reduce_scatter | solution.py:411
  1023.0 515.7 %reduce-scatter.32.cloned.1.call-start = ((), (), s32[]{:S(2)}) async-start(), calls=%async_computation.39 | async-start | bytes 14417920 | tf_op jit(solution)/shard_map/reduce_scatter | solution.py:414
  1034.5 994.9 %reduce-scatter.22.cloned.1.call-start = ((), (), s32[]{:S(2)}) async-start(), calls=%async_computation.34 | async-start | bytes 23789568 | tf_op jit(solution)/shard_map/reduce_scatter | solution.py:524
  1045.1 1475.3 %reduce-scatter.24.cloned.1.call-start = ((), (), s32[]{:S(2)}) async-start(), calls=%async_computation.35 | async-start | bytes 23789568 | tf_op jit(solution)/shard_map/reduce_scatter | solution.py:525
  1055.6 1955.7 %reduce-scatter.26.cloned.1.call-start = ((), (), s32[]{:S(2)}) async-start(), calls=%async_computation.36 | async-start | bytes 23789568 | tf_op jit(solution)/shard_map/reduce_scatter | solution.py:526
  1067.1 2303.6 %reduce-scatter.20.cloned.1.call-start = ((), (), s32[]{:S(2)}) async-start(), calls=%async_computation.33 | async-start | bytes 17301504 | tf_op jit(solution)/shard_map/reduce_scatter | solution.py:519
  1078.9 15.3 all-to-all-start.9
  1094.1 26.9 all-to-all-start.11
  1121.1 12.6 all-to-all-start.10
  1127.1 2498.0 %reduce-scatter.18.cloned.1.call-start = ((), (), s32[]{:S(2)}) async-start(), calls=%async_computation.32 | async-start | bytes 25952256 | tf_op jit(solution)/shard_map/reduce_scatter | solution.py:518
  1148.9 102.1 %copy-start.17 = (bf16[128,16,128]{0,2,1:T(8,128)(2,1)S(1)}, bf16[128,16,128]{0,2,1:T(8,128)(2,1)}, u32[]{:S(2)}) copy-start(bf16[128,16,128]{0,2,1:T(8,128)(2,1)} %copy-done.16) | copy-start | bytes 1572868
  (51 other events, 792.9 us)
Sparse Core Ops, SparseCore 0:
  11.0 97.5 all-gather.8
  128.2 16.8 all-gather.10
  146.7 16.7 all-gather.12
  166.3 80.4 all-gather.14
  249.4 159.0 all-gather.16
  411.2 120.3 all-gather.18
  534.4 126.4 all-gather.20
  994.8 95.4 reduce-scatter.15
  1093.6 24.8 reduce-scatter.13
  1121.2 128.3 reduce-scatter.33
  1252.4 96.4 reduce-scatter.27
  1351.5 92.1 reduce-scatter.29
  1446.5 92.1 reduce-scatter.31
  1541.5 487.9 reduce-scatter.21
  2032.3 488.0 reduce-scatter.23
  2523.2 488.0 reduce-scatter.25
  3014.1 356.5 reduce-scatter.19
  3378.7 246.3 reduce-scatter.17
where the time goes:
time: 3650 us; the launch traced here: 3630 us
  waiting for transfers between devices  2770 us (76%)
  blocking collectives  293 us (8%)
  matrix products  270 us (7%)
  local copies, waits for them, and re-layouts  141 us (4%)
  other arithmetic  71.6 us (2%)
  starting transfers between devices  68.5 us (2%)
    reduce_scatter x1, waiting for transfers between devices, body(): lax.psum_scatter(shared_up_grad, ('context', 'experts'), scatter_dimensio...  491 us
    reduce_scatter x1, waiting for transfers between devices, body(): lax.psum_scatter(shared_down_grad, ('context', 'experts'), scatter_dimens...  491 us
    reduce_scatter x1, waiting for transfers between devices, body(): lax.psum_scatter(shared_gate_grad, ('context', 'experts'), scatter_dimens...  486 us
    reduce_scatter x1, waiting for transfers between devices, body(): lax.psum_scatter(out_weight_grad, ('context', 'experts'), scatter_dimensi...  359 us
    reduce_scatter x1, waiting for transfers between devices, body(): lax.psum_scatter(qkv_weight_grad, ('context', 'experts'), scatter_dimensi...  254 us
    all_gather x1, blocking collectives, gather_dense(): lax.all_gather(shards[4], ('context', 'experts'), axis=0, tiled=True)  178 us
    all_to_all x1, waiting for transfers between devices, body(): lax.all_to_all(to_experts(routed_dy), 'experts', split_axis=0, concat_axi...  116 us
    unnamed x19, waiting for transfers between devices  96.4 us
  transfers between devices with their start and end apart: 28, of which 22 were waited for; matrix products, arithmetic and copies ran while one was open for 10% of the time, Pallas kernels for 0%

commit v1 on v0

v1 whole, which is shorter than its diff:
```python
import functools
import math

import jax
import jax.numpy as jnp
from jax import lax
from jax.experimental import pallas as pl
from jax.experimental.pallas import tpu as pltpu
from jax.sharding import PartitionSpec as P

QUERY_HEADS = 16
KEY_VALUE_HEADS = 4
HEAD_DIM = 128
TOP = 6


EPSILON = 1e-06
THETA = 10000.0
NEG_LARGE = -1e30


def rms_scale(values):
    return lax.rsqrt(jnp.mean(values * values, axis=-1, keepdims=True) + EPSILON)


def norm_back(values, row_scale, gain_values, grad_out):
    weighted = grad_out * gain_values
    gain_grad = jnp.sum(grad_out * values * row_scale, axis=0)
    inner_mean = jnp.mean(weighted * values, axis=-1, keepdims=True)
    return (
        row_scale * weighted - values * row_scale * row_scale * row_scale * inner_mean,
        gain_grad,
    )


def inner_rows(left, right):
    return lax.dot_general(
        left, right, (((0,), (0,)), ((), ())), preferred_element_type=jnp.float32
    )


def dot_last(left, right):
    return lax.dot_general(
        left, right, (((1,), (1,)), ((), ())), preferred_element_type=jnp.float32
    )


def ring_pairs(count):
    order = [i for i in range(count) if i % 2 == 0] + [i for i in reversed(range(count)) if i % 2 == 1]
    right = [(order[i], order[(i + 1) % count]) for i in range(count)]
    left = [(order[i], order[(i - 1) % count]) for i in range(count)]
    return right, left


def ring_place(index, count):
    return jnp.where(index % 2 == 0, index // 2, count - 1 - index // 2)


def ring_index(place, count):
    place = (place + 2 * count) % count
    return jnp.where(place < count // 2, 2 * place, 2 * (count - 1 - place) + 1)


class RingGather:
    def __init__(self, block):
        self.count = lax.axis_size("experts")
        self.right, self.left = ring_pairs(self.count)
        self.half = block.shape[0] // 2
        self.block = block
        self.ahead = [block]
        self.behind = [block]
        self.far = None

    def step(self):
        if len(self.ahead) < self.count // 2:
            self.behind.append(lax.ppermute(self.behind[-1], "experts", self.right))
            self.ahead.append(lax.ppermute(self.ahead[-1], "experts", self.left))
        else:
            self.far = [
                lax.ppermute(self.behind[-1][: self.half], "experts", self.right),
                lax.ppermute(self.ahead[-1][self.half :], "experts", self.left),
            ]

    def latest(self):
        return self.far if self.far else [self.behind[-1], self.ahead[-1]]

    def replace(self, values):
        if self.far:
            self.far = list(values)
        else:
            self.behind[-1], self.ahead[-1] = values

    def pieces(self):
        return self.ahead + self.far + self.behind[:0:-1]


class RingScatter:
    def __init__(self, whole):
        self.count = lax.axis_size("experts")
        self.right, self.left = ring_pairs(self.count)
        self.whole = whole
        self.rows = whole.shape[0] // self.count
        self.half = self.rows // 2
        self.left_steps = self.count // 2
        self.first = None
        self.second = None

    def own(self, step):
        start = step % self.count * self.rows
        return self.whole[start : start + self.rows].astype(jnp.float32)

    def arrived(self):
        first = self.first.astype(jnp.float32)
        second = self.second.astype(jnp.float32)
        if self.left_steps == self.count // 2 - 1:
            blank = jnp.zeros((self.half, self.whole.shape[1]), jnp.float32)
            first = jnp.concatenate([first, blank], axis=0)
            second = jnp.concatenate([blank, second], axis=0)
        return first, second

    def step(self):
        if self.first is None:
            far = self.own(self.left_steps)
            first, second = far[: self.half], far[self.half :]
        else:
            first, second = self.arrived()
            first = first + self.own(self.left_steps)
            second = second + self.own(-self.left_steps)
        self.first = lax.ppermute(first.astype(jnp.bfloat16), "experts", self.right)
        self.second = lax.ppermute(second.astype(jnp.bfloat16), "experts", self.left)
        self.left_steps -= 1

    def latest(self):
        return [self.first, self.second]

    def replace(self, values):
        self.first, self.second = values

    def total(self):
        first, second = self.arrived()
        return first + second + self.own(0)


def meet(rings, *values):
    held, values = lax.optimization_barrier(([ring.latest() for ring in rings], values))
    for ring, value in zip(rings, held):
        ring.replace(value)
    return values


def ring_order(values):
    count = lax.axis_size("experts")
    place = ring_place(lax.axis_index("experts"), count)
    return jnp.concatenate(
        [
            lax.dynamic_slice_in_dim(values, ring_index(place + step, count), 1, 0)
            for step in range(count)
        ],
        axis=0,
    )


def flip_pairs(count, bit):
    return [(i, i ^ bit) for i in range(count)]


def flip_gather(block, axis):
    count = lax.axis_size(axis)
    index = lax.axis_index(axis)
    whole = block[None]
    bit = 1
    while bit < count:
        received = lax.ppermute(whole, axis, flip_pairs(count, bit))
        whole = jnp.where(
            (index // bit) % 2 == 0,
            jnp.concatenate([whole, received], axis=0),
            jnp.concatenate([received, whole], axis=0),
        )
        bit *= 2
    return whole


def flip_scatter(values, axis):
    count = lax.axis_size(axis)
    index = lax.axis_index(axis)
    bit = 1
    while bit < count:
        pairs = values.reshape((values.shape[0] // 2, 2) + values.shape[1:])
        mine = (index // bit) % 2
        sent = lax.dynamic_index_in_dim(pairs, 1 - mine, 1, keepdims=False)
        kept = lax.dynamic_index_in_dim(pairs, mine, 1, keepdims=False)
        values = kept + lax.ppermute(sent, axis, flip_pairs(count, bit))
        bit *= 2
    return values[0]


def context_gather(block):
    count = lax.axis_size("context")
    index = lax.axis_index("context")
    whole = block[None]
    bit = count // 2
    while bit >= 1:
        received = lax.ppermute(whole, "context", flip_pairs(count, bit))
        low = (index // bit) % 2 == 0
        whole = jnp.stack(
            [jnp.where(low, whole, received), jnp.where(low, received, whole)], axis=1
        ).reshape((2 * whole.shape[0],) + block.shape)
        bit //= 2
    return whole.reshape(count * block.shape[0], block.shape[1])


def core_parts(piece_of):
    count = lax.axis_size("context")
    index = lax.axis_index("context")
    return {place: piece_of(index ^ (place + 1)) for place in range(count - 2, -1, -2)}


def core_exchange(parts):
    pairs = flip_pairs(lax.axis_size("context"), 1)
    return {
        place: lax.ppermute(part.astype(jnp.bfloat16), "context", pairs)
        for place, part in parts.items()
    }


def core_sums(piece_of, received):
    index = lax.axis_index("context")
    return {
        place // 2: piece_of(index ^ place, part) for place, part in received.items()
    }


def far_sums(pieces):
    count = lax.axis_size("context")
    bit = 2
    while bit < count:
        merged = {}
        for place in sorted(pieces, reverse=True):
            if place % 2 == 0:
                received = lax.ppermute(
                    pieces[place + 1].astype(jnp.bfloat16), "context", flip_pairs(count, bit)
                )
                merged[place // 2] = pieces[place] + received.astype(jnp.float32)
        pieces = merged
        bit *= 2
    return pieces[0]


def block_sums(values, received):
    def piece_of(target, part):
        return lax.dynamic_index_in_dim(values, target, 0, keepdims=False) + part.astype(jnp.float32)

    return core_sums(piece_of, received)


def block_parts(values):
    return core_parts(lambda target: lax.dynamic_index_in_dim(values, target, 0, keepdims=False))


def to_experts(stacked):
    return lax.all_to_all(stacked, "experts", split_axis=0, concat_axis=0, tiled=True)


VMEM_BYTES = 60 * 1024 * 1024


def kernel_options():
    return dict(
        compiler_params=pltpu.CompilerParams(vmem_limit_bytes=VMEM_BYTES),
        cost_estimate=pl.CostEstimate(flops=1024, bytes_accessed=1024, transcendentals=0),
    )


def in_vmem(count):
    return [pl.BlockSpec(memory_space=pltpu.VMEM)] * count


def in_smem(count):
    return [pl.BlockSpec(memory_space=pltpu.SMEM)] * count


def plain_dot(left, right):
    return jnp.dot(left, right, preferred_element_type=jnp.float32)


def last_dims(left, right):
    return lax.dot_general(
        left, right, (((1,), (1,)), ((), ())), preferred_element_type=jnp.float32
    )


def first_dims(left, right):
    return lax.dot_general(
        left, right, (((0,), (0,)), ((), ())), preferred_element_type=jnp.float32
    )


def project_kernel(piece_count, *refs):
    pieces = refs[:piece_count]
    gain_ref, weight_ref, cosine_ref, sine_ref, normed_ref, query_ref, key_value_ref = refs[piece_count:]
    start = 0
    for piece in pieces:
        rows = piece.shape[0]
        values = piece[...].astype(jnp.float32)
        scale = lax.rsqrt(jnp.mean(values * values, axis=-1, keepdims=True) + EPSILON)
        normed_ref[start : start + rows, :] = (values * scale * gain_ref[...]).astype(jnp.bfloat16)
        start += rows
    step = math.gcd(start, 512)
    query_width = query_ref.shape[1]

    @pl.loop(0, start // step)
    def _(index):
        here = pl.ds(pl.multiple_of(index * step, step), step)
        normed = normed_ref[here, :]
        cosine = cosine_ref[here, :]
        sine = sine_ref[here, :]

        def rotated(offset):
            head = heads[:, offset : offset + HEAD_DIM]
            return (head * cosine + pltpu.roll(head, HEAD_DIM // 2, 1) * sine).astype(jnp.bfloat16)

        heads = plain_dot(normed, weight_ref[:, :query_width])
        for offset in range(0, query_width, HEAD_DIM):
            query_ref[here, offset : offset + HEAD_DIM] = rotated(offset)
        heads = plain_dot(normed, weight_ref[:, query_width:])
        key_value_ref[here, :HEAD_DIM] = rotated(0)
        key_value_ref[here, HEAD_DIM:] = heads[:, HEAD_DIM:].astype(jnp.bfloat16)


def project(pieces, gain, weight, cosine, sine, query_width):
    rows = sum(piece.shape[0] for piece in pieces)
    width = pieces[0].shape[1]
    return pl.pallas_call(
        functools.partial(project_kernel, len(pieces)),
        out_shape=(
            jax.ShapeDtypeStruct((rows, width), jnp.bfloat16),
            jax.ShapeDtypeStruct((rows, query_width), jnp.bfloat16),
            jax.ShapeDtypeStruct((rows, weight.shape[1] - query_width), jnp.bfloat16),
        ),
        in_specs=in_vmem(len(pieces) + 4),
        out_specs=tuple(in_vmem(3)),
        **kernel_options(),
    )(*pieces, gain, weight, cosine, sine)


def stack_heads(values):
    heads = values.shape[1] // HEAD_DIM
    return jnp.concatenate(
        [values[:, i * HEAD_DIM : (i + 1) * HEAD_DIM] for i in range(heads)], axis=0
    )


def spread_heads(values, heads):
    rows = values.shape[0] // heads
    return jnp.concatenate([values[i * rows : (i + 1) * rows] for i in range(heads)], axis=1)


def stack_lanes(values):
    return jnp.concatenate([values[i : i + 1] for i in range(values.shape[0])], axis=1)


def visible_keys(shape, key_start, query_start, query_tile):
    key_pos = key_start + lax.broadcasted_iota(jnp.int32, shape, 0)
    query_pos = query_start + lax.rem(lax.broadcasted_iota(jnp.int32, shape, 1), query_tile)
    return query_pos >= key_pos


def ring_slices(order_ref, rows, first, count):
    spread = order_ref.shape[0]
    length = rows // spread
    found = []
    for i in range(count):
        number = first + i
        base = lax.div(number, spread) * rows
        place = order_ref[lax.rem(number, spread)] * length
        found.append(pl.ds(pl.multiple_of(base + place, length), length))
    return found


def forward_kernel(
    query_tile, key_tile, block_ref, order_ref, query_ref, key_value_ref, out_ref, low_ref, ring_ref, total_ref
):
    rows = query_ref.shape[0]
    length = rows // order_ref.shape[0]
    heads = query_ref.shape[1] // HEAD_DIM
    wide = heads * query_tile
    scale = HEAD_DIM ** (-0.5) * math.log2(math.e)

    @pl.loop(0, rows // query_tile)
    def _(index):
        offset = pl.multiple_of(index * query_tile, query_tile)
        places = ring_slices(order_ref, rows, index * (query_tile // length), query_tile // length)
        queries = stack_heads(jnp.concatenate([query_ref[place, :] for place in places], axis=0))
        start = block_ref[0] * rows + offset

        def step(tile, state, masked):
            top, total, summed = state
            here = ring_slices(order_ref, rows, tile * (key_tile // length), key_tile // length)
            keys = jnp.concatenate([key_value_ref[place, :HEAD_DIM] for place in here], axis=0)
            values = jnp.concatenate([key_value_ref[place, HEAD_DIM:] for place in here], axis=0)
            scores = last_dims(keys, queries) * scale
            if masked:
                seen = visible_keys(scores.shape, tile * key_tile, start, query_tile)
                scores = jnp.where(seen, scores, NEG_LARGE)
            new_top = jnp.maximum(top, jnp.max(scores, axis=0, keepdims=True))
            weights = jnp.exp2(scores - new_top)
            rescale = jnp.exp2(top - new_top)
            total = total * rescale + jnp.sum(weights, axis=0, keepdims=True)
            summed = summed * rescale + first_dims(values, weights.astype(jnp.bfloat16))
            return new_top, total, summed

        state = (
            jnp.full((1, wide), NEG_LARGE, jnp.float32),
            jnp.zeros((1, wide), jnp.float32),
            jnp.zeros((HEAD_DIM, wide), jnp.float32),
        )
        full = lax.div(start, key_tile)
        state = lax.fori_loop(0, full, lambda tile, state: step(tile, state, False), state)
        top, total, summed = step(full, state, True)
        result = spread_heads((summed / total).T, heads)
        out_ref[pl.ds(offset, query_tile), :] = result
        low = result.astype(jnp.bfloat16)
        low_ref[pl.ds(offset, query_tile), :] = low
        for i, place in enumerate(places):
            ring_ref[place, :] = low[i * length : (i + 1) * length]
        log_total = top + jnp.log2(total)
        for i in range(heads):
            total_ref[i : i + 1, pl.ds(offset, query_tile)] = log_total[
                :, i * query_tile : (i + 1) * query_tile
            ]


def backward_kernel(
    query_tile,
    key_tile,
    block_ref,
    order_ref,
    query_ref,
    key_value_ref,
    out_ref,
    grad_ref,
    total_ref,
    cosine_ref,
    sine_ref,
    query_grad_ref,
    key_value_grad_ref,
):
    rows = query_ref.shape[0]
    length = rows // order_ref.shape[0]
    heads = query_ref.shape[1] // HEAD_DIM
    wide = heads * query_tile
    score_scale = HEAD_DIM ** (-0.5)
    scale = score_scale * math.log2(math.e)

    @pl.loop(0, key_value_ref.shape[0] // key_tile)
    def _(tile):
        key_start = pl.multiple_of(tile * key_tile, key_tile)
        key_value_grad_ref[pl.ds(key_start, key_tile), :] = jnp.zeros(
            (key_tile, 2 * HEAD_DIM), jnp.float32
        )

    @pl.loop(0, rows // query_tile)
    def _(index):
        offset = pl.multiple_of(index * query_tile, query_tile)
        places = ring_slices(order_ref, rows, index * (query_tile // length), query_tile // length)
        queries = stack_heads(jnp.concatenate([query_ref[place, :] for place in places], axis=0))
        grads = stack_heads(grad_ref[pl.ds(offset, query_tile), :])
        outs = stack_heads(out_ref[pl.ds(offset, query_tile), :])
        delta = jnp.sum((grads.astype(jnp.float32) * outs).T, axis=0, keepdims=True)
        log_total = stack_lanes(total_ref[:, pl.ds(offset, query_tile)])
        start = block_ref[0] * rows + offset

        def step(tile, query_grad, masked):
            here = ring_slices(order_ref, rows, tile * (key_tile // length), key_tile // length)
            keys = jnp.concatenate([key_value_ref[place, :HEAD_DIM] for place in here], axis=0)
            values = jnp.concatenate([key_value_ref[place, HEAD_DIM:] for place in here], axis=0)
            weights = jnp.exp2(last_dims(keys, queries) * scale - log_total)
            if masked:
                seen = visible_keys(weights.shape, tile * key_tile, start, query_tile)
                weights = jnp.where(seen, weights, 0.0)
            value_part = plain_dot(weights.astype(jnp.bfloat16), grads)
            score_grad = (weights * (last_dims(values, grads) - delta)).astype(jnp.bfloat16)
            key_part = plain_dot(score_grad, queries) * score_scale
            part = jnp.concatenate([key_part, value_part], axis=1)
            for i, place in enumerate(here):
                key_value_grad_ref[place, :] += part[i * length : (i + 1) * length]
            return query_grad + first_dims(score_grad, keys)

        full = lax.div(start, key_tile)
        query_grad = lax.fori_loop(
            0,
            full,
            lambda tile, state: step(tile, state, False),
            jnp.zeros((wide, HEAD_DIM), jnp.float32),
        )
        query_grad = step(full, query_grad, True) * score_scale
        for i, place in enumerate(places):
            cosine = cosine_ref[place, :]
            sine = sine_ref[place, :]
            for head in range(heads):
                begin = head * query_tile + i * length
                part = query_grad[begin : begin + length]
                turned = part * cosine - pltpu.roll(part, HEAD_DIM // 2, 1) * sine
                query_grad_ref[place, head * HEAD_DIM : (head + 1) * HEAD_DIM] = turned.astype(
                    jnp.bfloat16
                )


def attention_forward(block_index, order, queries, keys):
    rows, wide = queries.shape
    return pl.pallas_call(
        functools.partial(forward_kernel, math.gcd(rows, 256), math.gcd(rows, 512)),
        out_shape=(
            jax.ShapeDtypeStruct((rows, wide), jnp.float32),
            jax.ShapeDtypeStruct((rows, wide), jnp.bfloat16),
            jax.ShapeDtypeStruct((rows, wide), jnp.bfloat16),
            jax.ShapeDtypeStruct((wide // HEAD_DIM, rows), jnp.float32),
        ),
        in_specs=in_smem(2) + in_vmem(2),
        out_specs=tuple(in_vmem(4)),
        **kernel_options(),
    )(block_index.reshape(1), order, queries, keys)


def attention_backward(block_index, order, queries, keys, outs, grads, log_total, cosine, sine):
    rows, wide = queries.shape
    return pl.pallas_call(
        functools.partial(backward_kernel, math.gcd(rows, 256), math.gcd(rows, 512)),
        out_shape=(
            jax.ShapeDtypeStruct((rows, wide), jnp.bfloat16),
            jax.ShapeDtypeStruct((keys.shape[0], 2 * HEAD_DIM), jnp.float32),
        ),
        in_specs=in_smem(2) + in_vmem(7),
        out_specs=tuple(in_vmem(2)),
        **kernel_options(),
    )(block_index.reshape(1), order, queries, keys, outs, grads, log_total, cosine, sine)


def dispatch_kernel(piece_count, experts, *refs):
    pieces = refs[:piece_count]
    chosen_ref, whole_ref, rows_ref = refs[piece_count:]
    start = 0
    for piece in pieces:
        whole_ref[start : start + piece.shape[0], :] = piece[...]
        start += piece.shape[0]
    length = chosen_ref.shape[2]
    capacity = chosen_ref.shape[1] // experts
    for block in range(chosen_ref.shape[0]):
        picked = plain_dot(chosen_ref[block], whole_ref[block * length : (block + 1) * length, :])
        picked = picked.astype(jnp.bfloat16)
        for expert in range(experts):
            rows_ref[expert, block * capacity : (block + 1) * capacity, :] = picked[
                expert * capacity : (expert + 1) * capacity
            ]


def dispatch(pieces, chosen, experts):
    rows = sum(piece.shape[0] for piece in pieces)
    width = pieces[0].shape[1]
    blocks, slots, _ = chosen.shape
    return pl.pallas_call(
        functools.partial(dispatch_kernel, len(pieces), experts),
        out_shape=(
            jax.ShapeDtypeStruct((rows, width), jnp.bfloat16),
            jax.ShapeDtypeStruct((experts, blocks * (slots // experts), width), jnp.bfloat16),
        ),
        in_specs=in_vmem(len(pieces) + 1),
        out_specs=tuple(in_vmem(2)),
        **kernel_options(),
    )(*pieces, chosen)


def column_tiles(width, tile, work):
    whole = width // tile

    @pl.loop(0, whole)
    def _(index):
        work(pl.ds(pl.multiple_of(index * tile, tile), tile))

    if width % tile:
        work(pl.ds(whole * tile, width % tile))


def expert_kernel(
    first_ref,
    rows_ref,
    grad_ref,
    gate_ref,
    weight_gate_ref,
    weight_up_ref,
    weight_down_ref,
    act_ref,
    gate_grad_ref,
    up_grad_ref,
    row_grad_ref,
    score_ref,
):
    hidden = act_ref.shape[2]
    width = rows_ref.shape[2]
    score_ref[...] = jnp.zeros_like(score_ref)

    def hidden_work(here):
        rows = rows_ref[0]
        pre_gate = plain_dot(rows, weight_gate_ref[0, :, here])
        pre_up = plain_dot(rows, weight_up_ref[0, :, here])
        act_grad = last_dims(grad_ref[0], weight_down_ref[0, here, :])
        sigmoid = 1.0 / (1.0 + jnp.exp(-pre_gate))
        silu = pre_gate * sigmoid
        act = (silu * pre_up).astype(jnp.bfloat16)
        act_ref[0, :, here] = act
        score_ref[...] += jnp.sum(act.astype(jnp.float32) * act_grad, axis=1, keepdims=True)
        act_grad = act_grad * gate_ref[0]
        gate_grad_ref[0, :, here] = (
            act_grad * pre_up * sigmoid * (1.0 + pre_gate * (1.0 - sigmoid))
        ).astype(jnp.bfloat16)
        up_grad_ref[0, :, here] = (act_grad * silu).astype(jnp.bfloat16)

    column_tiles(hidden, 256, hidden_work)

    @pl.loop(0, width // 256)
    def _(index):
        here = pl.ds(pl.multiple_of(index * 256, 256), 256)
        row_grad_ref[0, :, here] = (
            last_dims(gate_grad_ref[0], weight_gate_ref[0, here, :])
            + last_dims(up_grad_ref[0], weight_up_ref[0, here, :])
        ).astype(jnp.bfloat16)

    lane = lax.broadcasted_iota(jnp.int32, (score_ref.shape[0], HEAD_DIM), 1)
    own = first_ref[0] + pl.program_id(0)
    row_grad_ref[0, :, width:] = jnp.where(lane == own, score_ref[...], 0.0).astype(jnp.bfloat16)


def expert_pass(first_expert, rows, grads, gates, weight_gate, weight_up, weight_down):
    experts, count, width = rows.shape
    hidden = weight_gate.shape[2]

    def one(*shape):
        return pl.BlockSpec((1,) + shape, lambda expert: (expert, 0, 0))

    def low(*shape):
        return jax.ShapeDtypeStruct((experts,) + shape, jnp.bfloat16)

    return pl.pallas_call(
        expert_kernel,
        grid=(experts,),
        out_shape=(
            low(count, hidden),
            low(count, hidden),
            low(count, hidden),
            low(count, width + HEAD_DIM),
        ),
        in_specs=in_smem(1)
        + [
            one(count, width),
            one(count, width),
            one(count, 1),
            one(width, hidden),
            one(width, hidden),
            one(hidden, width),
        ],
        out_specs=(one(count, hidden), one(count, hidden), one(count, hidden), one(count, width + HEAD_DIM)),
        scratch_shapes=[pltpu.VMEM((count, 1), jnp.float32)],
        **kernel_options(),
    )(first_expert.reshape(1), rows, grads, gates, weight_gate, weight_up, weight_down)


def result_kernel(act_ref, gate_ref, weight_ref, out_ref):
    @pl.loop(0, out_ref.shape[2] // 256)
    def _(index):
        here = pl.ds(pl.multiple_of(index * 256, 256), 256)
        result = plain_dot(act_ref[0], weight_ref[0, :, here]).astype(jnp.bfloat16)
        out_ref[0, :, here] = (result.astype(jnp.float32) * gate_ref[0]).astype(jnp.bfloat16)


def expert_results(act, gates, weight_down):
    experts, count, hidden = act.shape
    width = weight_down.shape[2]

    def one(*shape):
        return pl.BlockSpec((1,) + shape, lambda expert: (expert, 0, 0))

    return pl.pallas_call(
        result_kernel,
        grid=(experts,),
        out_shape=jax.ShapeDtypeStruct((experts, count, width), jnp.bfloat16),
        in_specs=[one(count, hidden), one(count, 1), one(hidden, width)],
        out_specs=one(count, width),
        **kernel_options(),
    )(act, gates, weight_down)


def combine_kernel(turned, chosen_ref, values_ref, left_ref, right_ref, out_ref):
    width = right_ref.shape[0] if turned else right_ref.shape[1]
    experts = values_ref.shape[0]
    length = chosen_ref.shape[1]
    capacity = chosen_ref.shape[2] // experts
    blocks = chosen_ref.shape[0]

    def slots(block, here):
        part = 0.0
        for expert in range(experts):
            part = part + plain_dot(
                chosen_ref[block, :, expert * capacity : (expert + 1) * capacity],
                values_ref[expert, block * capacity : (block + 1) * capacity, here],
            )
        return part

    @pl.loop(0, width // 256)
    def _(index):
        here = pl.ds(pl.multiple_of(index * 256, 256), 256)
        shared = (
            last_dims(left_ref[...], right_ref[here, :])
            if turned
            else plain_dot(left_ref[...], right_ref[:, here])
        )
        for block in range(blocks):
            rows = slice(block * length, (block + 1) * length)
            out_ref[rows, here] = (shared[rows] + slots(block, here)).astype(jnp.bfloat16)

    if out_ref.shape[1] > width:
        for block in range(blocks):
            out_ref[block * length : (block + 1) * length, width:] = slots(
                block, slice(width, out_ref.shape[1])
            ).astype(jnp.bfloat16)


def combine(chosen, values, left, right, turned):
    blocks, length, slots = chosen.shape
    experts, _, wide = values.shape
    capacity = slots // experts
    some = math.gcd(blocks, 4)
    return pl.pallas_call(
        functools.partial(combine_kernel, turned),
        grid=(blocks // some,),
        out_shape=jax.ShapeDtypeStruct((blocks * length, wide), jnp.bfloat16),
        in_specs=[
            pl.BlockSpec((some, length, slots), lambda i: (i, 0, 0)),
            pl.BlockSpec((experts, some * capacity, wide), lambda i: (0, i, 0)),
            pl.BlockSpec((some * length, left.shape[1]), lambda i: (i, 0)),
            pl.BlockSpec(right.shape, lambda i: (0, 0)),
        ],
        out_specs=pl.BlockSpec((some * length, wide), lambda i: (i, 0)),
        **kernel_options(),
    )(chosen, values, left, right)


def shared_kernel(normed_ref, grad_ref, weight_ref, down_ref, act_ref, both_ref):
    hidden = act_ref.shape[1]
    pre_gate = plain_dot(normed_ref[...], weight_ref[:, :hidden])
    pre_up = plain_dot(normed_ref[...], weight_ref[:, hidden:])
    act_grad = last_dims(grad_ref[...], down_ref[...])
    sigmoid = 1.0 / (1.0 + jnp.exp(-pre_gate))
    silu = pre_gate * sigmoid
    act_ref[...] = (silu * pre_up).astype(jnp.bfloat16)
    both_ref[:, :hidden] = (
        act_grad * pre_up * sigmoid * (1.0 + pre_gate * (1.0 - sigmoid))
    ).astype(jnp.bfloat16)
    both_ref[:, hidden:] = (act_grad * silu).astype(jnp.bfloat16)


def shared_pass(normed, grads, weight, down):
    rows, width = normed.shape
    hidden = down.shape[0]
    some = math.gcd(rows, 256)

    def part(columns):
        return pl.BlockSpec((some, columns), lambda i: (i, 0))

    return pl.pallas_call(
        shared_kernel,
        grid=(rows // some,),
        out_shape=(
            jax.ShapeDtypeStruct((rows, hidden), jnp.bfloat16),
            jax.ShapeDtypeStruct((rows, 2 * hidden), jnp.bfloat16),
        ),
        in_specs=[
            part(width),
            part(width),
            pl.BlockSpec(weight.shape, lambda i: (0, 0)),
            pl.BlockSpec(down.shape, lambda i: (0, 0)),
        ],
        out_specs=(part(hidden), part(2 * hidden)),
        **kernel_options(),
    )(normed, grads, weight, down)


def piece_kernel(scaled, added, target_ref, left_ref, right_ref, *refs):
    right = right_ref[0]
    if scaled:
        right = (right.astype(jnp.float32) * refs[0][0]).astype(jnp.bfloat16)
    total = first_dims(left_ref[0], right)
    if added:
        total = total + refs[-2][0].astype(jnp.float32)
    refs[-1][0] = total.astype(jnp.bfloat16)


def weight_piece(target, left, right, parts, cut_left, gates=None, received=None):
    experts, count, left_width = left.shape
    right_width = right.shape[2]
    left_width, right_width = (
        (left_width // parts, right_width) if cut_left else (left_width, right_width // parts)
    )

    def spec(columns, cut):
        if cut:
            return pl.BlockSpec((1, count, columns), lambda e, t: (e, 0, t[0]))
        return pl.BlockSpec((1, count, columns), lambda e, t: (e, 0, 0))

    whole = pl.BlockSpec((1, left_width, right_width), lambda e, t: (e, 0, 0))
    operands = [left, right]
    specs = [spec(left_width, cut_left), spec(right_width, not cut_left)]
    if gates is not None:
        operands.append(gates)
        specs.append(pl.BlockSpec((1, count, 1), lambda e, t: (e, 0, 0)))
    if received is not None:
        operands.append(received)
        specs.append(whole)
    return pl.pallas_call(
        functools.partial(piece_kernel, gates is not None, received is not None),
        grid_spec=pltpu.PrefetchScalarGridSpec(
            num_scalar_prefetch=1, grid=(experts,), in_specs=specs, out_specs=whole
        ),
        out_shape=jax.ShapeDtypeStruct((experts, left_width, right_width), jnp.bfloat16),
        **kernel_options(),
    )(target.reshape(1), *operands)


def weight_sum_kernel(piece_count, left_ref, *refs):
    pieces = refs[:piece_count]
    out_ref = refs[piece_count]

    @pl.loop(0, out_ref.shape[1] // 256)
    def _(index):
        here = pl.ds(pl.multiple_of(index * 256, 256), 256)
        right = jnp.concatenate([piece[:, here] for piece in pieces], axis=0)
        out_ref[:, here] = first_dims(left_ref[...], right).astype(jnp.bfloat16)


def weight_sum(left, pieces):
    return pl.pallas_call(
        functools.partial(weight_sum_kernel, len(pieces)),
        out_shape=jax.ShapeDtypeStruct((left.shape[1], pieces[0].shape[1]), jnp.bfloat16),
        in_specs=in_vmem(len(pieces) + 1),
        out_specs=pl.BlockSpec(memory_space=pltpu.VMEM),
        **kernel_options(),
    )(left, *pieces)


def body(
    tokens,
    attn_gain,
    query_key_value_weight,
    out_weight,
    ffn_gain,
    router_weight,
    shared_gate,
    shared_up,
    shared_down,
    routed_gate_weight,
    routed_up_weight,
    routed_down_weight,
    routes,
    cotangent,
):
    f32 = jnp.float32
    bf16 = jnp.bfloat16
    both = ("context", "experts")
    context_count = lax.axis_size("context")
    spread = lax.axis_size("experts")
    context_index = lax.axis_index("context")
    expert_index = lax.axis_index("experts")
    token_count, width = tokens.shape
    local_experts = routed_gate_weight.shape[0]
    experts_all = local_experts * spread
    rows = token_count * spread
    weight_rows = query_key_value_weight.shape[0]
    query_width = QUERY_HEADS * HEAD_DIM
    key_width = KEY_VALUE_HEADS * HEAD_DIM
    repeat_times = spread // KEY_VALUE_HEADS
    head_share = QUERY_HEADS // spread
    own_width = head_share * HEAD_DIM
    block_width = width // context_count

    def key_columns(weight):
        heads = weight.reshape(weight_rows, KEY_VALUE_HEADS, HEAD_DIM)
        return jnp.repeat(heads, repeat_times, axis=1)

    qkv_send = jnp.concatenate(
        [
            query_key_value_weight[:, :query_width].reshape(weight_rows, spread, own_width),
            key_columns(query_key_value_weight[:, query_width : query_width + key_width]),
            key_columns(query_key_value_weight[:, query_width + key_width :]),
        ],
        axis=2,
    ).transpose(1, 0, 2)
    hidden_piece = shared_down.shape[0]
    hidden_own = hidden_piece * context_count
    hidden_wide = -(-hidden_own // HEAD_DIM) * HEAD_DIM

    def hidden_columns(weight):
        own_columns = (
            weight.reshape(weight_rows, context_count, spread, hidden_piece)
            .transpose(2, 0, 1, 3)
            .reshape(spread, weight_rows, hidden_own)
        )
        return jnp.pad(own_columns, ((0, 0), (0, 0), (0, hidden_wide - hidden_own)))

    shared_send = jnp.concatenate([hidden_columns(shared_gate), hidden_columns(shared_up)], axis=2)

    token_ring = RingGather(tokens)
    token_ring.step()
    qkv_rows = to_experts(qkv_send).reshape(spread * weight_rows, -1)
    small = jnp.concatenate([attn_gain[None], ffn_gain[None], router_weight.T], axis=0)
    small = flip_gather(small, "experts")
    qkv_rows, small = meet([token_ring], qkv_rows, small)
    token_ring.step()
    small = flip_gather(small, "context").transpose(2, 0, 1, 3).reshape(-1, width)
    gain_one = small[0].astype(f32)
    gain_two = small[1].astype(f32)
    router_full = small[2:]
    routes_block = flip_gather(routes.T, "experts")
    position = context_index * rows + jnp.arange(rows, dtype=jnp.int32)
    position = ring_order(position.reshape(spread, token_count)).reshape(rows).astype(f32)
    half_width = HEAD_DIM // 2
    frequency = THETA ** (-jnp.arange(half_width, dtype=f32) * 2.0 / HEAD_DIM)
    angles = position[:, None] * frequency[None, :]
    cosine = jnp.cos(angles)
    sine = jnp.sin(angles)
    cosine = jnp.concatenate([cosine, cosine], axis=1)
    sine = jnp.concatenate([-sine, sine], axis=1)
    qkv_own = context_gather(qkv_rows)
    gain_one, cosine, sine = meet([token_ring], gain_one, cosine, sine)
    token_ring.step()
    qkv_own, routes_block = meet([token_ring], qkv_own, routes_block)
    token_ring.step()
    out_weight, shared_send, shared_down, cotangent_late = meet(
        [token_ring], out_weight, shared_send, shared_down, cotangent
    )

    normed_one, query_rows, key_value = project(
        token_ring.pieces(), gain_one[None], qkv_own, cosine, sine, own_width
    )
    out_full = lax.all_gather(out_weight, both, axis=0, tiled=True)
    key_value, cotangent_late = lax.optimization_barrier((key_value, cotangent_late))
    grad_ring = RingGather(cotangent_late)
    grad_ring.step()
    key_value = context_gather(key_value)
    (key_value,) = meet([grad_ring], key_value)
    grad_ring.step()
    place = ring_place(expert_index, spread)
    order = (ring_place(jnp.arange(spread, dtype=jnp.int32), spread) - place + spread) % spread
    attended, attended_low, attended_ring, log_total = attention_forward(
        context_index, order, query_rows, key_value
    )
    (attended_low,) = meet([grad_ring], attended_low)
    grad_ring.step()
    attended_tok = (
        to_experts(attended_low.reshape(spread, token_count, own_width))
        .transpose(1, 0, 2)
        .reshape(token_count, query_width)
    )
    (attended_tok,) = meet([grad_ring], attended_tok)
    grad_ring.step()

    inputs = tokens.astype(f32)
    middle = inputs + jnp.dot(attended_tok, out_full, preferred_element_type=f32)
    (middle,) = meet([grad_ring], middle)
    scale_two = rms_scale(middle)
    normed_two = (middle * scale_two * gain_two).astype(bf16)
    normed_ring = RingGather(normed_two)
    normed_ring.step()

    first_expert = expert_index * local_experts
    own_ids = first_expert + jnp.arange(local_experts, dtype=jnp.int32)
    routes_block = ring_order(routes_block)
    member = jnp.any(routes_block[:, None] == own_ids[None, :, None, None], axis=2)
    counted = member.astype(jnp.int32)
    slot_index = jnp.cumsum(counted, axis=2) - counted
    capacity = token_count * TOP * 4 // (3 * experts_all)
    slot = jnp.arange(capacity, dtype=jnp.int32)
    chosen = member[:, :, None, :] & (slot_index[:, :, None, :] == slot[None, None, :, None])
    chosen_wide = chosen.astype(f32)
    slots = local_experts * capacity
    chosen_low = chosen.astype(bf16).reshape(spread, slots, token_count)
    chosen_back = chosen_low.transpose(0, 2, 1)
    grad_block, grad_rows = dispatch(grad_ring.pieces(), chosen_low, local_experts)
    shared_rows = to_experts(shared_send).reshape(spread * weight_rows, -1)
    shared_rows, grad_block, chosen_back = meet([normed_ring], shared_rows, grad_block, chosen_back)
    normed_ring.step()
    down_own = jnp.pad(context_gather(shared_down), ((0, hidden_wide - hidden_own), (0, 0)))
    (down_own,) = meet([normed_ring], down_own)
    normed_ring.step()
    shared_own = context_gather(shared_rows)
    (shared_own,) = meet([normed_ring], shared_own)
    normed_ring.step()
    meet([normed_ring])
    normed_block, expert_rows = dispatch(normed_ring.pieces(), chosen_low, local_experts)

    router_probs = jax.nn.softmax(dot_last(normed_block, router_full), axis=-1)
    gate_tokens = (
        lax.dynamic_slice_in_dim(router_probs, first_expert, local_experts, 1)
        .reshape(spread, token_count, local_experts)
        .transpose(0, 2, 1)
    )
    gates = jnp.sum(chosen_wide * gate_tokens[:, :, None, :], axis=3)
    gates = gates.transpose(1, 0, 2).reshape(local_experts, spread * capacity, 1)
    act, expert_dg, expert_du, row_grad = expert_pass(
        first_expert,
        expert_rows,
        grad_rows,
        gates,
        routed_gate_weight,
        routed_up_weight,
        routed_down_weight,
    )
    shared_act, shared_both = shared_pass(normed_block, grad_block, shared_own, down_own)
    grad_scatter = RingScatter(combine(chosen_back, row_grad, shared_both, shared_own, True))

    def down_piece(target, received=None):
        return weight_piece(target, act, grad_rows, context_count, False, gates, received)

    def gate_piece(target, received=None):
        return weight_piece(target, expert_rows, expert_dg, context_count, True, None, received)

    def up_piece(target, received=None):
        return weight_piece(target, expert_rows, expert_du, context_count, True, None, received)

    grad_scatter.step()
    down_parts = core_parts(down_piece)
    (down_parts,) = meet([grad_scatter], down_parts)
    grad_scatter.step()
    down_sums = core_sums(down_piece, core_exchange(down_parts))
    gate_parts = core_parts(gate_piece)
    down_sums, gate_parts = meet([grad_scatter], down_sums, gate_parts)
    grad_scatter.step()
    gate_sums = core_sums(gate_piece, core_exchange(gate_parts))
    up_parts = core_parts(up_piece)
    gate_sums, up_parts = meet([grad_scatter], gate_sums, up_parts)
    grad_scatter.step()
    up_sums = core_sums(up_piece, core_exchange(up_parts))
    shared_sum = inner_rows(normed_block, shared_both).astype(bf16)
    shared_sum = shared_sum.reshape(context_count, block_width, -1)
    up_sums, shared_sum = meet([grad_scatter], up_sums, shared_sum)
    gathered = grad_scatter.total()

    prob_grad = gathered[:, width : width + experts_all]
    probs_tok = router_probs[:token_count]
    logit_grad = (
        probs_tok * (prob_grad - jnp.sum(probs_tok * prob_grad, axis=-1, keepdims=True))
    ).astype(bf16)
    normed_grad = gathered[:, :width] + jnp.dot(
        logit_grad, router_full, preferred_element_type=f32
    )
    grad_final = cotangent.astype(f32)
    middle_norm_grad, ffn_gain_part = norm_back(middle, scale_two, gain_two, normed_grad)
    middle_grad = grad_final + middle_norm_grad
    branch_grad = middle_grad.astype(bf16)
    attended_grad = dot_last(branch_grad, out_full).astype(bf16)
    branch_ring = RingGather(branch_grad)
    branch_ring.step()
    grad_heads = to_experts(
        attended_grad.reshape(token_count, spread, own_width).transpose(1, 0, 2)
    ).reshape(rows, own_width)
    weighted_y = expert_results(act, gates, routed_down_weight)
    out_scatter = RingScatter(combine(chosen_back, weighted_y, shared_act, down_own, False))
    shared_received = core_exchange(block_parts(shared_sum))
    shared_down_sum = inner_rows(shared_act, grad_block)[:hidden_own].astype(bf16)
    shared_down_sum = shared_down_sum.reshape(context_count, hidden_piece, width)
    shared_down_received = core_exchange(block_parts(shared_down_sum))
    expert_down_grad = far_sums(down_sums)
    grad_heads, expert_down_grad, shared_received, shared_down_received = meet(
        [branch_ring], grad_heads, expert_down_grad, shared_received, shared_down_received
    )

    branch_ring.step()
    out_scatter.step()
    query_grad, key_value_all = attention_backward(
        context_index,
        order,
        query_rows,
        key_value,
        attended,
        grad_heads,
        log_total,
        cosine,
        sine,
    )
    shared_far = far_sums(block_sums(shared_sum, shared_received))
    key_value_all, shared_far = meet([branch_ring, out_scatter], key_value_all, shared_far)
    branch_ring.step()
    out_scatter.step()
    key_value_all = key_value_all.reshape(context_count, rows, -1)
    key_value_sums = block_sums(key_value_all, core_exchange(block_parts(key_value_all)))
    shared_back = to_experts(shared_far.astype(bf16).reshape(spread, weight_rows, -1))
    (key_value_sums,) = meet([branch_ring, out_scatter], key_value_sums)
    branch_ring.step()
    out_scatter.step()
    key_value_grad = far_sums(key_value_sums)
    shared_down_grad = far_sums(block_sums(shared_down_sum, shared_down_received))
    small_part = jnp.concatenate([ffn_gain_part[None], inner_rows(logit_grad, normed_two)], axis=0)
    small_part = small_part.reshape(-1, context_count, spread, weight_rows).transpose(1, 2, 0, 3)
    small_sum = flip_scatter(small_part, "context")
    key_value_grad, shared_down_grad, small_sum, shared_back = meet(
        [branch_ring, out_scatter], key_value_grad, shared_down_grad, small_sum, shared_back
    )
    expert_gate_grad = far_sums(gate_sums)
    key_grad = key_value_grad[:, :HEAD_DIM]
    turned = jnp.concatenate([key_grad[:, half_width:], key_grad[:, :half_width]], axis=1)
    key_value_pre = jnp.concatenate(
        [key_grad * cosine - turned * sine, key_value_grad[:, HEAD_DIM:]], axis=1
    ).astype(bf16)
    projected_grad = jnp.concatenate([query_grad, key_value_pre], axis=1)
    projected_grad, expert_gate_grad = lax.optimization_barrier((projected_grad, expert_gate_grad))
    input_scatter = RingScatter(dot_last(projected_grad, qkv_own).astype(bf16))
    input_scatter.step()
    out_scatter.step()
    qkv_sum = inner_rows(normed_one, projected_grad).astype(bf16)
    qkv_sum = qkv_sum.reshape(context_count, block_width, -1)
    qkv_received = core_exchange(block_parts(qkv_sum))
    out_sum = weight_sum(attended_ring, branch_ring.pieces())
    out_sum = out_sum.reshape(context_count, own_width // context_count, width)
    out_received = core_exchange(block_parts(out_sum))
    qkv_received, out_received = meet([input_scatter, out_scatter], qkv_received, out_received)
    input_scatter.step()
    qkv_far = far_sums(block_sums(qkv_sum, qkv_received))
    out_own = far_sums(block_sums(out_sum, out_received))
    small_sum = flip_scatter(small_sum, "experts")
    qkv_far, out_own, small_sum = meet([input_scatter], qkv_far, out_own, small_sum)
    ffn_gain_grad = small_sum[0]
    router_weight_grad = small_sum[1:].T
    input_scatter.step()
    qkv_back = to_experts(qkv_far.astype(bf16).reshape(spread, weight_rows, -1))
    out_weight_grad = lax.ppermute(
        out_own.astype(bf16),
        both,
        [
            (i * spread + j, j * context_count + i)
            for i in range(context_count)
            for j in range(spread)
        ],
    ).astype(f32)
    layer_out = (middle + out_scatter.total()[:, :width]).astype(bf16)
    qkv_back, out_weight_grad, layer_out = meet(
        [input_scatter], qkv_back, out_weight_grad, layer_out
    )
    input_scatter.step()

    def hidden_home(values):
        return (
            values.astype(f32)
            .reshape(spread, weight_rows, context_count, hidden_piece)
            .transpose(1, 2, 0, 3)
            .reshape(weight_rows, -1)
        )

    shared_gate_grad = hidden_home(shared_back[:, :, :hidden_own])
    shared_up_grad = hidden_home(shared_back[:, :, hidden_wide : hidden_wide + hidden_own])

    def key_home(values):
        return (
            values.reshape(KEY_VALUE_HEADS, repeat_times, weight_rows, HEAD_DIM)
            .sum(axis=1)
            .transpose(1, 0, 2)
            .reshape(weight_rows, key_width)
        )

    qkv_back = qkv_back.astype(f32)
    qkv_weight_grad = jnp.concatenate(
        [
            qkv_back[:, :, :own_width].transpose(1, 0, 2).reshape(weight_rows, query_width),
            key_home(qkv_back[:, :, own_width : own_width + HEAD_DIM]),
            key_home(qkv_back[:, :, own_width + HEAD_DIM :]),
        ],
        axis=1,
    )
    attn_gain_grad = jnp.sum(
        query_key_value_weight.astype(f32) * qkv_weight_grad, axis=1
    ) / attn_gain.astype(f32)
    expert_up_grad = far_sums(up_sums)
    input_norm_grad, _ = norm_back(inputs, rms_scale(inputs), gain_one, input_scatter.total())
    tokens_grad = middle_grad + input_norm_grad
    return (
        layer_out,
        tokens_grad,
        attn_gain_grad,
        qkv_weight_grad,
        out_weight_grad,
        ffn_gain_grad,
        router_weight_grad,
        shared_gate_grad,
        shared_up_grad,
        shared_down_grad,
        expert_gate_grad,
        expert_up_grad,
        expert_down_grad,
    )


def solution(mesh):
    return jax.shard_map(
        body,
        mesh=mesh,
        in_specs=(
            P(("context", "experts"), None),
            P(("context", "experts")),
            P(("context", "experts"), None),
            P(("context", "experts"), None),
            P(("context", "experts")),
            P(("context", "experts"), None),
            P(("context", "experts"), None),
            P(("context", "experts"), None),
            P(("context", "experts"), None),
            P("experts", None, None),
            P("experts", None, None),
            P("experts", None, None),
            P(("context", "experts"), None),
            P(("context", "experts"), None),
        ),
        out_specs=(
            P(("context", "experts"), None),
            P(("context", "experts"), None),
            P(("context", "experts")),
            P(("context", "experts"), None),
            P(("context", "experts"), None),
            P(("context", "experts")),
            P(("context", "experts"), None),
            P(("context", "experts"), None),
            P(("context", "experts"), None),
            P(("context", "experts"), None),
            P("experts", "context", None),
            P("experts", "context", None),
            P("experts", None, "context"),
        ),
        check_vma=False,
    )
```

time: 3650 us -> 924 us (0.25)
  waiting for transfers between devices: 2770 us -> 340 us
  blocking collectives: 293 us -> 0 us
  matrix products: 270 us -> 33.1 us
  Pallas kernels: 0 us -> 206 us
  starting transfers between devices: 68.5 us -> 170 us
  local copies, waits for them, and re-layouts: 141 us -> 60.3 us
    reduce_scatter x10 -> x0, waiting for transfers between devices: 2320 us -> none  [the longest x1 491 us: body(): lax.psum_scatter(shared_up_grad, ('context', 'experts'), scatter_dimensio...]
    ppermute x0 -> x102, waiting for transfers between devices: none -> 325 us  [the longest x8 139 us: far_sums(): lax.ppermute(pieces[place + 1].astype(jnp.bfloat16), 'context', flip_pair...]
    all_to_all x10 -> x6, waiting for transfers between devices: 247 us -> 14.4 us  [to_experts(): lax.all_to_all(stacked, 'experts', split_axis=0, concat_axis=0, tiled=True)]
    pallas_call x0 -> x23, Pallas kernels: none -> 206 us  [the longest x12 59.5 us: weight_piece(): pl.pallas_call(functools.partial(piece_kernel, gates is not None, receive...]
    all_gather x1 -> x0, blocking collectives: 178 us -> none  [gather_dense(): lax.all_gather(shards[4], ('context', 'experts'), axis=0, tiled=True)]
    dot_general x29 -> x2, matrix products: 178 us -> 6.12 us  [the longest x1 4.74 us: body(): jnp.dot(attended_tok, out_full, preferred_element_type=f32)]
    ppermute x0 -> x102, starting transfers between devices: none -> 130 us  [the longest x8 22.3 us: flip_gather(): received = lax.ppermute(whole, axis, flip_pairs(count, bit))]
    all_gather x7 -> x1, waiting for transfers between devices: 106 us -> 0.01 us  [body(): out_full = lax.all_gather(out_weight, both, axis=0, tiled=True)]
  transfers between devices with their start and end apart: 28 -> 109, of which waited for: 22 -> 35; matrix products, arithmetic and copies ran while one was open for 10% -> 17% of each run, Pallas kernels for 0% -> 14%
where the time goes in v1:
time: 924 us; the launch traced here: 914 us
  waiting for transfers between devices  340 us (37%)
  Pallas kernels  206 us (22%)
  starting transfers between devices  170 us (18%)
  other arithmetic  89.3 us (10%)
  local copies, waits for them, and re-layouts  60.3 us (7%)
  matrix products  33.1 us (4%)
  between operations  15.8 us (2%)
    ppermute x8, waiting for transfers between devices, far_sums(): lax.ppermute(pieces[place + 1].astype(jnp.bfloat16), 'context', flip_pair...  139 us
    ppermute x12, waiting for transfers between devices, step(): self.behind.append(lax.ppermute(self.behind[-1], 'experts', self.right))  66.2 us
    pallas_call x12, Pallas kernels, weight_piece(): pl.pallas_call(functools.partial(piece_kernel, gates is not None, receive...  59.5 us
    pallas_call x1, Pallas kernels, expert_pass(): pl.pallas_call(expert_kernel, grid=(experts,), out_shape=(low(count, hidd...  49.7 us
    all_to_all x6, starting transfers between devices, to_experts(): lax.all_to_all(stacked, 'experts', split_axis=0, concat_axis=0, tiled=True)  39.8 us
    ppermute x8, waiting for transfers between devices, context_gather(): received = lax.ppermute(whole, 'context', flip_pairs(count, bit))  39.3 us
    pallas_call x2, Pallas kernels, combine(): pl.pallas_call(functools.partial(combine_kernel, turned), grid=(blocks //...  24.5 us
    add x8, other arithmetic, far_sums(): merged[place // 2] = pieces[place] + received.astype(jnp.float32)  24.1 us
  transfers between devices with their start and end apart: 109, of which 35 were waited for; matrix products, arithmetic and copies ran while one was open for 17% of the time, Pallas kernels for 14%

profile of v1, /device:TPU:10, one launch (start us, length us, event | category | flops | bytes accessed | tf_op | source)
XLA Modules:
  0.0 914.0 jit_solution(14015391423101837764)
XLA Ops:
  22.5 12.9 %collective-permute-start.3 = (bf16[2,18,64]{2,1,0:T(8,128)(2,1)S(1)}, bf16[2,18,64]{2,1,0:T(8,128)(2,1)S(1)}, u32[]{:S(2)}, u32[]{:S(2)}) collective-permute-start(bf16[2,18,64]{2,1,0:T(8,128)(2,1)S(1)} %maximum_select_fusion.4), channel_id=1, source_target_pairs={{0,2},{1,3},{2,0},{3,1},{4,6},{5,7},{6,4},{7,5},{8,10},{9,11},{10,... | collective-permute-start | bytes 13832 | tf_op jit(solution)/shard_map/ppermute | solution.py:173
  44.1 10.7 %collective-permute-done.11 = bf16[1,512,512]{2,1,0:T(8,128)(2,1)S(1)} collective-permute-done((bf16[1,512,512]{2,1,0:T(8,128)(2,1)S(1)}, bf16[1,512,512]{2,1,0:T(8,128)(2,1)S(1)}, u32[]{:S(2)}, u32[]{:S(2)}) %collective-permute-start.11) | collective-permute-done | bytes 524320 | tf_op jit(solution)/shard_map/ppermute | solution.py:203
  64.2 10.5 %collective-permute-done.14 = s32[2,6,128]{2,1,0:T(8,128)S(1)} collective-permute-done((s32[2,6,128]{2,1,0:T(8,128)S(1)}, s32[2,6,128]{2,1,0:T(8,128)S(1)}, u32[]{:S(2)}, u32[]{:S(2)}) %collective-permute-start.14) | collective-permute-done | bytes 6176 | tf_op jit(solution)/shard_map/ppermute | solution.py:173
  83.0 8.2 collective-permute-done.9.refs_6_
  102.4 8.4 shard_map.237
  112.3 11.3 %collective-permute-done.20 = bf16[1,1024,256]{2,1,0:T(8,128)(2,1)S(1)} collective-permute-done((bf16[1,1024,256]{2,1,0:T(8,128)(2,1)}, bf16[1,1024,256]{2,1,0:T(8,128)(2,1)S(1)}, u32[]{:S(2)}, u32[]{:S(2)}) %collective-permute-start.20) | collective-permute-done | bytes 524320 | tf_op jit(solution)/shard_map/ppermute | solution.py:203
  129.3 19.5 %collective-permute-done.18.refs_8_ = bf16[128,2048]{1,0:T(8,128)(2,1)S(1)} collective-permute-done((bf16[128,2048]{1,0:T(8,128)(2,1)S(1)}, bf16[128,2048]{1,0:T(8,128)(2,1)S(1)}, u32[]{:S(2)}, u32[]{:S(2)}) %collective-permute-start.18) | collective-permute-done | bytes 524320 | tf_op jit(solution)/shard_map/ppermute | solution.py:76
  152.7 7.5 shard_map.238
  160.2 13.0 %collective-permute-done.22.refs_7_ = bf16[128,2048]{1,0:T(8,128)(2,1)S(1)} collective-permute-done((bf16[128,2048]{1,0:T(8,128)(2,1)S(1)}, bf16[128,2048]{1,0:T(8,128)(2,1)S(1)}, u32[]{:S(2)}, u32[]{:S(2)}) %collective-permute-start.22) | collective-permute-done | bytes 524320 | tf_op jit(solution)/shard_map/ppermute | solution.py:76
  175.4 9.9 %all-to-all-start.1 = ((bf16[8,128,256]{1,2,0:T(8,128)(2,1)}), bf16[8,128,256]{1,2,0:T(8,128)(2,1)S(1)}, u32[]{:S(2)}, u32[]{:S(2)}) async-start(bf16[8,128,256]{1,2,0:T(8,128)(2,1)} %copy.258), calls=%async_computation.1 | async-start | bytes 1048576 | tf_op jit(solution)/shard_map/all_to_all | solution.py:261
  188.1 14.4 %all-to-all-done.1 = bf16[8,128,256]{1,2,0:T(8,128)(2,1)S(1)} async-done(((bf16[8,128,256]{1,2,0:T(8,128)(2,1)}), bf16[8,128,256]{1,2,0:T(8,128)(2,1)S(1)}, u32[]{:S(2)}, u32[]{:S(2)}) %all-to-all-start.1) | async-done | bytes 524320 | tf_op jit(solution)/shard_map/all_to_all | solution.py:261
  207.6 8.3 collective-permute-done.24.refs_6_
  238.8 6.5 shard_map.239
  248.1 15.0 %collective-permute-done.36 = bf16[1,512,768]{2,1,0:T(8,128)(2,1)S(1)} collective-permute-done((bf16[1,512,768]{2,1,0:T(8,128)(2,1)S(1)}, bf16[1,512,768]{2,1,0:T(8,128)(2,1)S(1)}, u32[]{:S(2)}, u32[]{:S(2)}) %collective-permute-start.36) | collective-permute-done | bytes 786464 | tf_op jit(solution)/shard_map/ppermute | solution.py:203
  269.5 8.6 collective-permute-done.30.refs_7_
  282.5 8.7 collective-permute-done.34.refs_6_
  300.2 6.7 shard_map.240
  313.1 11.0 %shard_map.242 = (bf16[1024,384]{1,0:T(8,128)(2,1)}, bf16[1024,768]{1,0:T(8,128)(2,1)}) custom-call(bf16[1024,2048]{1,0:T(8,128)(2,1)} %get-tuple-element.197.normed_ref, bf16[1024,2048]{1,0:T(8,128)(2,1)} %get-tuple-element.199.grad_ref, bf16[2048,768]{1,0:T(8,128)(2,1)} %bitcast.253, bf16[384,2048]{1,0:T(8,128)(2,1)} %pad.25.down_ref.right_ref), custom_call_target="tpu_custom_call" | custom-call | flops 1024 | bytes 1024 | tf_op jit(solution)/shard_map/pallas_call | solution.py:769
  324.2 49.7 %shard_map.241 = (bf16[2,512,1408]{2,1,0:T(8,128)(2,1)}, bf16[2,512,1408]{2,1,0:T(8,128)(2,1)}, bf16[2,512,1408]{2,1,0:T(8,128)(2,1)}, bf16[2,512,2176]{2,1,0:T(8,128)(2,1)}) custom-call(s32[1]{0:T(128)} %bitcast.40.first_ref, bf16[2,512,2048]{2,1,0:T(8,128)(2,1)} %get-tuple-element.195.rows_ref.left_ref, ...), custom_call_target="tpu_custom_call" | custom-call | flops 1024 | bytes 1024 | tf_op jit(solution)/shard_map/pallas_call | solution.py:643
  373.9 13.5 %shard_map.243 = bf16[1024,2176]{1,0:T(8,128)(2,1)} custom-call(bf16[8,128,128]{2,1,0:T(8,128)(2,1)} %bitcast.263, bf16[2,512,2176]{2,1,0:T(8,128)(2,1)} %get-tuple-element.198.values_ref, bf16[1024,768]{1,0:T(8,128)(2,1)} %get-tuple-element.202.left_ref, bf16[2048,768]{1,0:T(8,128)(2,1)} %bitcast.254), custom_call_target="tpu_custom_call" | custom-call | flops 1024 | bytes 1024 | tf_op jit(solution)/shard_map/pallas_call | solution.py:732
  450.6 14.1 %shard_map.257.values_ref = bf16[2,512,2048]{2,1,0:T(8,128)(2,1)} custom-call(bf16[2,512,1408]{2,1,0:T(8,128)(2,1)} %get-tuple-element.203.left_ref.act_ref, f32[2,512,1]{2,1,0:T(8,128)} %reshape.359.gate_ref.refs_0_, bf16[2,1408,2048]{2,1,0:T(8,128)(2,1)} %weight_ref.1), custom_call_target="tpu_custom_call" | custom-call | flops 1024 | bytes 1024 | tf_op jit(solution)/shard_map/pallas_call | solution.py:682
  464.7 11.1 %shard_map.258 = bf16[1024,2048]{1,0:T(8,128)(2,1)} custom-call(bf16[8,128,128]{2,1,0:T(8,128)(2,1)} %bitcast.264, bf16[2,512,2048]{2,1,0:T(8,128)(2,1)} %shard_map.257.values_ref, bf16[1024,384]{1,0:T(8,128)(2,1)} %get-tuple-element.223.left_ref, bf16[384,2048]{1,0:T(8,128)(2,1)} %pad.25.down_ref.right_ref), custom_call_target="tpu_custom_call" | custom-call | flops 1024 | bytes 1024 | tf_op jit(solution)/shard_map/pallas_call | solution.py:732
  511.4 6.6 convolution_convert_fusion.3
  529.5 21.1 %collective-permute-done.56 = bf16[2,1408,512]{2,1,0:T(8,128)(2,1)} collective-permute-done((bf16[2,1408,512]{2,1,0:T(8,128)(2,1)}, bf16[2,1408,512]{2,1,0:T(8,128)(2,1)}, u32[]{:S(2)}, u32[]{:S(2)}) %collective-permute-start.56) | collective-permute-done | bytes 2883616 | tf_op jit(solution)/shard_map/ppermute | solution.py:240
  568.2 44.2 %collective-permute-done.80 = bf16[2,512,1408]{2,1,0:T(8,128)(2,1)} collective-permute-done((bf16[2,512,1408]{2,1,0:T(8,128)(2,1)}, bf16[2,512,1408]{2,1,0:T(8,128)(2,1)}, u32[]{:S(2)}, u32[]{:S(2)}) %collective-permute-start.80) | collective-permute-done | bytes 2883616 | tf_op jit(solution)/shard_map/ppermute | solution.py:240
  621.2 11.6 %shard_map.256 = (bf16[1024,256]{1,0:T(8,128)(2,1)}, f32[4096,256]{1,0:T(8,128)}) custom-call(s32[1]{0:T(128)} %bitcast.block_ref.target_ref, s32[8]{0:T(128)} %and_select_fusion.order_ref, bf16[1024,256]{1,0:T(8,128)(2,1)} %get-tuple-element.161.query_ref, bf16[4096,256]{1,0:T(8,128)(2,1)} %bitcast.256, f32[1024,256]{1,0:T(8,128)} %get-tuple-element.167.out_ref, ...), custom_call_target="tpu_custom_call" | custom-call | flops 1024 | bytes 1024 | tf_op jit(solution)/shard_map/pallas_call | solution.py:527
  632.8 16.4 %collective-permute-start.79 = (f32[1,8,17,64]{3,1,2,0:T(8,128)S(1)}, f32[1,8,17,64]{3,1,2,0:T(8,128)S(1)}, u32[]{:S(2)}, u32[]{:S(2)}) collective-permute-start(f32[1,8,17,64]{3,1,2,0:T(8,128)S(1)} %constant_dynamic-slice_fusion.6), channel_id=1, source_target_pairs={{0,16},{8,24},{16,0},{24,8},{1,17},{9,25},{17,1},{25,9},{2,18},{10... | collective-permute-start | bytes 104456 | tf_op jit(solution)/shard_map/ppermute | solution.py:192
  679.9 8.3 collective-permute-done.68
  694.6 55.0 %collective-permute-done.77 = bf16[88,2048]{1,0:T(8,128)(2,1)S(1)} collective-permute-done((bf16[88,2048]{1,0:T(8,128)(2,1)S(1)}, bf16[88,2048]{1,0:T(8,128)(2,1)S(1)}, u32[]{:S(2)}, u32[]{:S(2)}) %collective-permute-start.77) | collective-permute-done | bytes 360480 | tf_op jit(solution)/shard_map/ppermute | solution.py:240
  831.7 12.8 %collective-permute-done.92 = bf16[64,2048]{1,0:T(8,128)(2,1)S(1)} collective-permute-done((bf16[64,2048]{1,0:T(8,128)(2,1)S(1)}, bf16[64,2048]{1,0:T(8,128)(2,1)S(1)}, u32[]{:S(2)}, u32[]{:S(2)}) %collective-permute-start.92) | collective-permute-done | bytes 262176 | tf_op jit(solution)/shard_map/ppermute | solution.py:240
  862.9 22.0 %collective-permute-done.98 = bf16[64,2048]{1,0:T(8,128)(2,1)S(1)} collective-permute-done((bf16[64,2048]{1,0:T(8,128)(2,1)S(1)}, bf16[64,2048]{1,0:T(8,128)(2,1)S(1)}, u32[]{:S(2)}, u32[]{:S(2)}) %collective-permute-start.98) | collective-permute-done | bytes 262176 | tf_op jit(solution)/shard_map/ppermute | solution.py:1133
  890.8 11.8 %collective-permute-done.100 = bf16[128,2048]{1,0:T(8,128)(2,1)S(1)} collective-permute-done((bf16[128,2048]{1,0:T(8,128)(2,1)S(1)}, bf16[128,2048]{1,0:T(8,128)(2,1)S(1)}, u32[]{:S(2)}, u32[]{:S(2)}) %collective-permute-start.100) | collective-permute-done | bytes 524320 | tf_op jit(solution)/shard_map/ppermute | solution.py:130
  (553 shorter events, 409.2 us)
Async XLA Ops:
  10.4 32.0 %all-to-all-start = ((bf16[8,64,512]{2,1,0:T(8,128)(2,1)}), bf16[8,64,512]{2,1,0:T(8,128)(2,1)S(1)}, u32[]{:S(2)}, u32[]{:S(2)}) async-start(bf16[8,64,512]{2,1,0:T(8,128)(2,1)} %copy.253), calls=%async_computation | async-start | bytes 1048576 | tf_op jit(solution)/shard_map/all_to_all | solution.py:261
  16.7 202.7 %all-gather.2.cloned.1.call-start = ((), (), s32[]{:S(2)}) async-start(), calls=%async_computation.6 | async-start | bytes 8650752 | tf_op jit(solution)/shard_map/all_gather | solution.py:943
  186.0 29.9 %collective-permute-start.24 = (bf16[128,2048]{1,0:T(8,128)(2,1)S(1)}, bf16[128,2048]{1,0:T(8,128)(2,1)S(1)}, u32[]{:S(2)}, u32[]{:S(2)}) collective-permute-start(bf16[128,2048]{1,0:T(8,128)(2,1)S(1)} %collective-permute-done.22.refs_7_), channel_id=1, source_target_pairs={{0,2},{2,4},{4,6},{6,7},{7,5},{5,3},{3,1},{1,0},{8,10},{10,12},{12... | collective-permute-start | bytes 1572872 | tf_op jit(solution)/shard_map/ppermute | solution.py:76
  186.6 29.3 %collective-permute-start.25 = (bf16[128,2048]{1,0:T(8,128)(2,1)}, bf16[128,2048]{1,0:T(8,128)(2,1)S(1)}, u32[]{:S(2)}, u32[]{:S(2)}) collective-permute-start(bf16[128,2048]{1,0:T(8,128)(2,1)} %collective-permute-done.23.refs_2_), channel_id=1, source_target_pairs={{0,1},{2,0},{4,2},{6,4},{7,6},{5,7},{3,5},{1,3},{8,9},{10,8},{12,1... | collective-permute-start | bytes 1572872 | tf_op jit(solution)/shard_map/ppermute | solution.py:77
  202.5 42.9 %all-to-all-start.2 = ((bf16[8,64,768]{2,1,0:T(8,128)(2,1)}), bf16[8,64,768]{2,1,0:T(8,128)(2,1)S(1)}, u32[]{:S(2)}, u32[]{:S(2)}) async-start(bf16[8,64,768]{2,1,0:T(8,128)(2,1)} %fusion.13), calls=%async_computation.2 | async-start | bytes 1572864 | tf_op jit(solution)/shard_map/all_to_all | solution.py:261
  450.0 43.6 %collective-permute-start.52 = (bf16[2,512,1408]{2,1,0:T(8,128)(2,1)}, bf16[2,512,1408]{2,1,0:T(8,128)(2,1)}, u32[]{:S(2)}, u32[]{:S(2)}) collective-permute-start(bf16[2,512,1408]{2,1,0:T(8,128)(2,1)} %shard_map.252), channel_id=1, source_target_pairs={{0,8},{8,0},{16,24},{24,16},{1,9},{9,1},{17,25},{25,17},{2,10},{10... | collective-permute-start | bytes 8650760 | tf_op jit(solution)/shard_map/ppermute | solution.py:221
  450.1 48.7 %collective-permute-start.53 = (bf16[2,512,1408]{2,1,0:T(8,128)(2,1)}, bf16[2,512,1408]{2,1,0:T(8,128)(2,1)}, u32[]{:S(2)}, u32[]{:S(2)}) collective-permute-start(bf16[2,512,1408]{2,1,0:T(8,128)(2,1)} %shard_map.253), channel_id=1, source_target_pairs={{0,8},{8,0},{16,24},{24,16},{1,9},{9,1},{17,25},{25,17},{2,10},{10... | collective-permute-start | bytes 8650760 | tf_op jit(solution)/shard_map/ppermute | solution.py:221
  484.9 65.7 %collective-permute-start.56 = (bf16[2,1408,512]{2,1,0:T(8,128)(2,1)}, bf16[2,1408,512]{2,1,0:T(8,128)(2,1)}, u32[]{:S(2)}, u32[]{:S(2)}) collective-permute-start(bf16[2,1408,512]{2,1,0:T(8,128)(2,1)} %shard_map.247), channel_id=1, source_target_pairs={{0,16},{8,24},{16,0},{24,8},{1,17},{9,25},{17,1},{25,9},{2,18},{10... | collective-permute-start | bytes 8650760 | tf_op jit(solution)/shard_map/ppermute | solution.py:240
  493.6 34.4 %collective-permute-start.59 = (bf16[88,2048]{1,0:T(8,128)(2,1)}, bf16[88,2048]{1,0:T(8,128)(2,1)}, u32[]{:S(2)}, u32[]{:S(2)}) collective-permute-start(bf16[88,2048]{1,0:T(8,128)(2,1)} %get-tuple-element.328), channel_id=1, source_target_pairs={{0,8},{8,0},{16,24},{24,16},{1,9},{9,1},{17,25},{25,17},{2,10},{10... | collective-permute-start | bytes 1081352 | tf_op jit(solution)/shard_map/ppermute | solution.py:221
  498.9 30.6 %collective-permute-start.60 = (bf16[88,2048]{1,0:T(8,128)(2,1)}, bf16[88,2048]{1,0:T(8,128)(2,1)}, u32[]{:S(2)}, u32[]{:S(2)}) collective-permute-start(bf16[88,2048]{1,0:T(8,128)(2,1)} %get-tuple-element.327), channel_id=1, source_target_pairs={{0,8},{8,0},{16,24},{24,16},{1,9},{9,1},{17,25},{25,17},{2,10},{10... | collective-permute-start | bytes 1081352 | tf_op jit(solution)/shard_map/ppermute | solution.py:221
  504.5 107.8 %collective-permute-start.80 = (bf16[2,512,1408]{2,1,0:T(8,128)(2,1)}, bf16[2,512,1408]{2,1,0:T(8,128)(2,1)}, u32[]{:S(2)}, u32[]{:S(2)}) collective-permute-start(bf16[2,512,1408]{2,1,0:T(8,128)(2,1)} %shard_map.251), channel_id=1, source_target_pairs={{0,16},{8,24},{16,0},{24,8},{1,17},{9,25},{17,1},{25,9},{2,18},{10... | collective-permute-start | bytes 8650760 | tf_op jit(solution)/shard_map/ppermute | solution.py:240
  510.6 51.9 %collective-permute-start.54 = (bf16[128,2048]{1,0:T(8,128)(2,1)}, bf16[128,2048]{1,0:T(8,128)(2,1)}, u32[]{:S(2)}, u32[]{:S(2)}) collective-permute-start(bf16[128,2048]{1,0:T(8,128)(2,1)} %fusion.34.refs_0_), channel_id=1, source_target_pairs={{0,2},{2,4},{4,6},{6,7},{7,5},{5,3},{3,1},{1,0},{8,10},{10,12},{12... | collective-permute-start | bytes 1572872 | tf_op jit(solution)/shard_map/ppermute | solution.py:76
  518.8 45.6 %all-to-all-start.3 = ((bf16[8,128,256]{2,1,0:T(8,128)(2,1)}), bf16[8,128,256]{2,1,0:T(8,128)(2,1)}, u32[]{:S(2)}, u32[]{:S(2)}) async-start(bf16[8,128,256]{2,1,0:T(8,128)(2,1)} %bitcast.288), calls=%async_computation.3 | async-start | bytes 1048576 | tf_op jit(solution)/shard_map/all_to_all | solution.py:261
  528.0 35.0 %collective-permute-start.55 = (bf16[128,2048]{1,0:T(8,128)(2,1)}, bf16[128,2048]{1,0:T(8,128)(2,1)}, u32[]{:S(2)}, u32[]{:S(2)}) collective-permute-start(bf16[128,2048]{1,0:T(8,128)(2,1)} %fusion.34.refs_0_), channel_id=1, source_target_pairs={{0,1},{2,0},{4,2},{6,4},{7,6},{5,7},{3,5},{1,3},{8,9},{10,8},{12,1... | collective-permute-start | bytes 1572872 | tf_op jit(solution)/shard_map/ppermute | solution.py:77
  529.5 35.0 %collective-permute-start.57 = (bf16[512,768]{1,0:T(8,128)(2,1)}, bf16[512,768]{1,0:T(8,128)(2,1)}, u32[]{:S(2)}, u32[]{:S(2)}) collective-permute-start(bf16[512,768]{1,0:T(8,128)(2,1)} %get-tuple-element.316), channel_id=1, source_target_pairs={{0,8},{8,0},{16,24},{24,16},{1,9},{9,1},{17,25},{25,17},{2,10},{10... | collective-permute-start | bytes 2359304 | tf_op jit(solution)/shard_map/ppermute | solution.py:221
  562.4 89.6 %collective-permute-start.63 = (bf16[64,2048]{1,0:T(8,128)(2,1)}, bf16[64,2048]{1,0:T(8,128)(2,1)}, u32[]{:S(2)}, u32[]{:S(2)}) collective-permute-start(bf16[64,2048]{1,0:T(8,128)(2,1)} %get-tuple-element.314), channel_id=1, source_target_pairs={{0,2},{2,4},{4,6},{6,7},{7,5},{5,3},{3,1},{1,0},{8,10},{10,12},{12... | collective-permute-start | bytes 786440 | tf_op jit(solution)/shard_map/ppermute | solution.py:129
  563.1 88.9 %collective-permute-start.64 = (bf16[64,2048]{1,0:T(8,128)(2,1)}, bf16[64,2048]{1,0:T(8,128)(2,1)}, u32[]{:S(2)}, u32[]{:S(2)}) collective-permute-start(bf16[64,2048]{1,0:T(8,128)(2,1)} %get-tuple-element.313), channel_id=1, source_target_pairs={{0,1},{2,0},{4,2},{6,4},{7,6},{5,7},{3,5},{1,3},{8,9},{10,8},{12,1... | collective-permute-start | bytes 786440 | tf_op jit(solution)/shard_map/ppermute | solution.py:130
  564.5 54.4 %collective-permute-start.78 = (f32[2,8,17,64]{3,1,2,0:T(8,128)}, f32[2,8,17,64]{3,1,2,0:T(8,128)}, u32[]{:S(2)}, u32[]{:S(2)}) collective-permute-start(f32[2,8,17,64]{3,1,2,0:T(8,128)} %bitcast.251), channel_id=1, source_target_pairs={{0,8},{8,0},{16,24},{24,16},{1,9},{9,1},{17,25},{25,17},{2,10},{10... | collective-permute-start | bytes 208904 | tf_op jit(solution)/shard_map/ppermute | solution.py:192
  566.9 65.9 %collective-permute-start.65 = (bf16[512,768]{1,0:T(8,128)(2,1)}, bf16[512,768]{1,0:T(8,128)(2,1)}, u32[]{:S(2)}, u32[]{:S(2)}) collective-permute-start(bf16[512,768]{1,0:T(8,128)(2,1)} %fusion), channel_id=1, source_target_pairs={{0,16},{8,24},{16,0},{24,8},{1,17},{9,25},{17,1},{25,9},{2,18},{10... | collective-permute-start | bytes 2359304 | tf_op jit(solution)/shard_map/ppermute | solution.py:240
  618.2 33.8 %collective-permute-start.61 = (bf16[128,2048]{1,0:T(8,128)(2,1)}, bf16[128,2048]{1,0:T(8,128)(2,1)}, u32[]{:S(2)}, u32[]{:S(2)}) collective-permute-start(bf16[128,2048]{1,0:T(8,128)(2,1)} %collective-permute-done.54.refs_8_), channel_id=1, source_target_pairs={{0,2},{2,4},{4,6},{6,7},{7,5},{5,3},{3,1},{1,0},{8,10},{10,12},{12... | collective-permute-start | bytes 1572872 | tf_op jit(solution)/shard_map/ppermute | solution.py:76
  618.8 33.2 %collective-permute-start.62 = (bf16[128,2048]{1,0:T(8,128)(2,1)}, bf16[128,2048]{1,0:T(8,128)(2,1)}, u32[]{:S(2)}, u32[]{:S(2)}) collective-permute-start(bf16[128,2048]{1,0:T(8,128)(2,1)} %collective-permute-done.55.refs_1_), channel_id=1, source_target_pairs={{0,1},{2,0},{4,2},{6,4},{7,6},{5,7},{3,5},{1,3},{8,9},{10,8},{12,1... | collective-permute-start | bytes 1572872 | tf_op jit(solution)/shard_map/ppermute | solution.py:77
  668.5 100.2 %all-to-all-start.4 = ((bf16[8,64,768]{2,1,0:T(8,128)(2,1)}), bf16[8,64,768]{2,1,0:T(8,128)(2,1)}, u32[]{:S(2)}, u32[]{:S(2)}) async-start(bf16[8,64,768]{2,1,0:T(8,128)(2,1)} %bitcast.274), calls=%async_computation.4 | async-start | bytes 1572864 | tf_op jit(solution)/shard_map/all_to_all | solution.py:261
  676.2 126.7 %collective-permute-start.101 = (bf16[2,512,1408]{2,1,0:T(8,128)(2,1)}, bf16[2,512,1408]{2,1,0:T(8,128)(2,1)}, u32[]{:S(2)}, u32[]{:S(2)}) collective-permute-start(bf16[2,512,1408]{2,1,0:T(8,128)(2,1)} %shard_map.255), channel_id=1, source_target_pairs={{0,16},{8,24},{16,0},{24,8},{1,17},{9,25},{17,1},{25,9},{2,18},{10... | collective-permute-start | bytes 8650760 | tf_op jit(solution)/shard_map/ppermute | solution.py:240
  678.1 71.4 %collective-permute-start.77 = (bf16[88,2048]{1,0:T(8,128)(2,1)S(1)}, bf16[88,2048]{1,0:T(8,128)(2,1)S(1)}, u32[]{:S(2)}, u32[]{:S(2)}) collective-permute-start(bf16[88,2048]{1,0:T(8,128)(2,1)S(1)} %copy-done.47), channel_id=1, source_target_pairs={{0,16},{8,24},{16,0},{24,8},{1,17},{9,25},{17,1},{25,9},{2,18},{10... | collective-permute-start | bytes 1081352 | tf_op jit(solution)/shard_map/ppermute | solution.py:240
  689.3 70.8 %collective-permute-start.76 = (bf16[1024,256]{1,0:T(8,128)(2,1)S(1)}, bf16[1024,256]{1,0:T(8,128)(2,1)S(1)}, u32[]{:S(2)}, u32[]{:S(2)}) collective-permute-start(bf16[1024,256]{1,0:T(8,128)(2,1)S(1)} %bitcast_add_fusion), channel_id=1, source_target_pairs={{0,16},{8,24},{16,0},{24,8},{1,17},{9,25},{17,1},{25,9},{2,18},{10... | collective-permute-start | bytes 1572872 | tf_op jit(solution)/shard_map/ppermute | solution.py:240
  691.5 76.6 %collective-permute-start.74 = (bf16[128,2048]{1,0:T(8,128)(2,1)S(1)}, bf16[128,2048]{1,0:T(8,128)(2,1)}, u32[]{:S(2)}, u32[]{:S(2)}) collective-permute-start(bf16[128,2048]{1,0:T(8,128)(2,1)S(1)} %get-tuple-element.308), channel_id=1, source_target_pairs={{0,2},{2,4},{4,6},{6,7},{7,5},{5,3},{3,1},{1,0},{8,10},{10,12},{12... | collective-permute-start | bytes 1572872 | tf_op jit(solution)/shard_map/ppermute | solution.py:129
  692.2 76.6 %collective-permute-start.75 = (bf16[128,2048]{1,0:T(8,128)(2,1)S(1)}, bf16[128,2048]{1,0:T(8,128)(2,1)}, u32[]{:S(2)}, u32[]{:S(2)}) collective-permute-start(bf16[128,2048]{1,0:T(8,128)(2,1)S(1)} %get-tuple-element.307), channel_id=1, source_target_pairs={{0,1},{2,0},{4,2},{6,4},{7,6},{5,7},{3,5},{1,3},{8,9},{10,8},{12,1... | collective-permute-start | bytes 1572872 | tf_op jit(solution)/shard_map/ppermute | solution.py:130
  775.5 27.5 %collective-permute-start.81 = (bf16[64,2048]{1,0:T(8,128)(2,1)S(1)}, bf16[64,2048]{1,0:T(8,128)(2,1)S(1)}, u32[]{:S(2)}, u32[]{:S(2)}) collective-permute-start(bf16[64,2048]{1,0:T(8,128)(2,1)S(1)} %get-tuple-element.306), channel_id=1, source_target_pairs={{0,2},{2,4},{4,6},{6,7},{7,5},{5,3},{3,1},{1,0},{8,10},{10,12},{12... | collective-permute-start | bytes 786440 | tf_op jit(solution)/shard_map/ppermute | solution.py:129
  781.1 42.4 %collective-permute-start.83 = (bf16[128,2048]{1,0:T(8,128)(2,1)}, bf16[128,2048]{1,0:T(8,128)(2,1)}, u32[]{:S(2)}, u32[]{:S(2)}) collective-permute-start(bf16[128,2048]{1,0:T(8,128)(2,1)} %get-tuple-element.304), channel_id=1, source_target_pairs={{0,2},{2,4},{4,6},{6,7},{7,5},{5,3},{3,1},{1,0},{8,10},{10,12},{12... | collective-permute-start | bytes 1572872 | tf_op jit(solution)/shard_map/ppermute | solution.py:129
  849.4 36.3 %collective-permute-start.96 = (bf16[128,2048]{1,0:T(8,128)(2,1)}, bf16[128,2048]{1,0:T(8,128)(2,1)S(1)}, u32[]{:S(2)}, u32[]{:S(2)}) collective-permute-start(bf16[128,2048]{1,0:T(8,128)(2,1)} %get-tuple-element.300), channel_id=1, source_target_pairs={{0,2},{2,4},{4,6},{6,7},{7,5},{5,3},{3,1},{1,0},{8,10},{10,12},{12... | collective-permute-start | bytes 1572872 | tf_op jit(solution)/shard_map/ppermute | solution.py:129
  851.4 34.4 %collective-permute-start.97 = (bf16[128,2048]{1,0:T(8,128)(2,1)}, bf16[128,2048]{1,0:T(8,128)(2,1)}, u32[]{:S(2)}, u32[]{:S(2)}) collective-permute-start(bf16[128,2048]{1,0:T(8,128)(2,1)} %get-tuple-element.299), channel_id=1, source_target_pairs={{0,1},{2,0},{4,2},{6,4},{7,6},{5,7},{3,5},{1,3},{8,9},{10,8},{12,1... | collective-permute-start | bytes 1572872 | tf_op jit(solution)/shard_map/ppermute | solution.py:130
  851.4 34.3 %all-to-all-start.5 = ((bf16[8,64,512]{2,1,0:T(8,128)(2,1)}), bf16[8,64,512]{2,1,0:T(8,128)(2,1)S(1)}, u32[]{:S(2)}, u32[]{:S(2)}) async-start(bf16[8,64,512]{2,1,0:T(8,128)(2,1)} %bitcast.103), calls=%async_computation.5 | async-start | bytes 1048576 | tf_op jit(solution)/shard_map/all_to_all | solution.py:261
  (153 other events, 2291.7 us)
Sparse Core Ops, SparseCore 0:
  101.8 100.9 all-gather.1
